TPU v7x, 32 devices: a whole 2x2x4 slice. The times are simulated.
32 devices in a mesh: ctx: 8 (over z, core), exp: 4 (over y, x).
Axes of the slice: x: 2, y: 2, z: 4, core: 2. Of those that a mesh axis runs over, the one named last changes fastest.
Arguments:
- tokens: bfloat16 [4, 2048, 1536], P('exp', 'ctx'), may hold values from -6 to 6
- cotangent: bfloat16 [4, 2048, 1536], P('exp', 'ctx'), may hold values from -6 to 6
- routes: int32 [4, 2048, 2], P('exp', 'ctx'), may hold values from 0 to 15, all different within a row; in each aligned block of 256 rows (0 to 255, 256 to 511, ..., all dimensions but the last counted through in order) at most 48 rows name the same one
- lengths: int32 [4, 3], P('exp'), may hold values from 1 to 1024, 2048 in all within a row
- block_order: int32 [4, 16], P('exp'), may hold values from 0 to 15, each once within a row
- gain_attn: float32 [1536], P(('ctx', 'exp')), may hold values from 0.5 to 1.5
- qkv_weight: float32 [1536, 2560], P(('ctx', 'exp')), may hold values from -0.15625 to 0.15625
- out_weight: float32 [1536, 1536], P(('ctx', 'exp')), may hold values from -1.5 to 1.5
- gain_moe: float32 [1536], P(('ctx', 'exp')), may hold values from 0.5 to 1.5
- router_weight: float32 [1536, 16], P(('ctx', 'exp')), may hold values from -0.109375 to 0.109375
- expert_in: float32 [16, 1536, 2048], P('exp', 'ctx'), may hold values from -0.15625 to 0.15625
- expert_out: float32 [16, 1024, 1536], P('exp', 'ctx'), may hold values from -0.375 to 0.375
Outputs:
- block_out: bfloat16 [4, 2048, 1536], P('exp', 'ctx')
- d_tokens: bfloat16 [4, 2048, 1536], P('exp', 'ctx')
- d_gain_attn: float32 [1536], P(('ctx', 'exp'))
- d_qkv_weight: float32 [1536, 2560], P(('ctx', 'exp'))
- d_out_weight: float32 [1536, 1536], P(('ctx', 'exp'))
- d_gain_moe: float32 [1536], P(('ctx', 'exp'))
- d_router_weight: float32 [1536, 16], P(('ctx', 'exp'))
- d_expert_in: float32 [16, 1536, 2048], P('exp', 'ctx')
- d_expert_out: float32 [16, 1024, 1536], P('exp', 'ctx')
Inputs may be any that keep to these rules, and one draw needn't show every extreme that they name: `routes`: among the rows of one device no expert is named more than 48 times; the two experts of a row differ. The lengths of a pack sum to 2048; the longest is 1024. `block_order`: each row is a permutation.
All inputs are finite; a program needn't handle non-finite values.
Results may differ from a plain program's by a relative error of at most 0.025.
Values may be sent and summed in bfloat16 or wider, within the bound.
A program may use at most 256 MiB of HBM per device.

v0:
```python
import functools

import jax
import jax.numpy as jnp
from jax import lax
from jax.experimental import pallas as pl
from jax.experimental.pallas import tpu as pltpu
from jax.sharding import Mesh
from jax.sharding import PartitionSpec as P

D = 1536
HEADS = 24
KV_HEADS = 8
HEAD = 64
GROUP = HEADS // KV_HEADS
FF = 1024
EXPERTS = 16
BLK = 128
CAP = 48
AUX = 128

epsilon = 1e-05
far_negative = -1e30
start_max = -1e29
F32 = jnp.float32
BF16 = jnp.bfloat16


def norm_scale(values):
    return lax.rsqrt(jnp.mean(values * values, axis=-1, keepdims=True) + epsilon)


def dot(a, b, dims=((1,), (0,))):
    return lax.dot_general(a, b, (dims, ((), ())), preferred_element_type=F32)


def lane_half(shape, half):
    lane = lax.broadcasted_iota(jnp.int32, shape, 1)
    return (lane >= HEAD) if half else (lane < HEAD)


def head_tiles(ref, rows, pair, scale):
    tiles = []
    for i in range(2 * GROUP):
        head = pair * 2 * GROUP + i
        group = head // GROUP
        tile = ref[rows, (head // 2) * 128 : (head // 2 + 1) * 128].astype(F32)
        if head % 2 != group % 2:
            tile = pltpu.roll(tile, HEAD, 1)
        tile = jnp.where(lane_half(tile.shape, group % 2), tile * scale, 0.0)
        tiles.append(tile.astype(BF16))
    return jnp.concatenate(tiles, axis=0)


def block_visibility(lengths_ref, query_block, key_block, parts):
    lanes = lax.broadcasted_iota(jnp.int32, (1, BLK), 1)
    query_pos = query_block * BLK + lanes
    start = jnp.zeros((1, BLK), jnp.int32)
    bound = jnp.int32(0)
    for s in range(parts - 1):
        bound = bound + lengths_ref[0, s]
        start = jnp.where(query_pos >= bound, bound, start)
    key_pos = key_block * BLK + lax.broadcasted_iota(jnp.int32, (BLK, BLK), 0)
    one = ((key_pos >= start) & (key_pos <= query_pos)).astype(jnp.int32)
    return jnp.concatenate([one] * (2 * GROUP), axis=1) > 0


def first_row_start(lengths_ref, query_block, parts):
    start = jnp.int32(0)
    bound = jnp.int32(0)
    for s in range(parts - 1):
        bound = bound + lengths_ref[0, s]
        start = jnp.where(query_block * BLK >= bound, bound, start)
    return start


def attend_blocks(
    parts,
    skip,
    lengths_ref,
    order_ref,
    mine,
    q_ref,
    kv_ref,
    exact_ref,
    out_ref,
    lse_ref,
    q_s,
    m_s,
    sum_s,
    acc_s,
):
    width = KV_HEADS * HEAD
    wide = 2 * GROUP * BLK
    for qb in range(q_ref.shape[0] // BLK):
        rows = pl.ds(qb * BLK, BLK)
        for pair in range(KV_HEADS // 2):
            q_s[pair] = head_tiles(q_ref, rows, pair, HEAD**-0.5)
            m_s[pair] = jnp.full((8, wide), start_max, F32)
            sum_s[pair] = jnp.zeros((8, wide), F32)
            acc_s[pair] = jnp.zeros((BLK, wide), F32)
        query_block = order_ref[0, mine + qb]
        first = first_row_start(lengths_ref, query_block, parts)

        @pl.loop(0, order_ref.shape[1])
        def _(kb):
            key_block = order_ref[0, kb]

            def fold():
                seen = block_visibility(lengths_ref, query_block, key_block, parts)
                key_rows = pl.ds(kb * BLK, BLK)
                for pair in range(KV_HEADS // 2):
                    keys = kv_ref[key_rows, pl.ds(pair * 128, 128)]
                    values = kv_ref[key_rows, pl.ds(width + pair * 128, 128)]
                    scores = dot(keys, q_s[pair], ((1,), (1,)))
                    scores = jnp.where(seen, scores, far_negative)
                    old = m_s[pair, 0:1, :]
                    new = jnp.maximum(old, jnp.max(scores, axis=0, keepdims=True))
                    weights = jnp.exp(scores - new)
                    factor = jnp.exp(old - new)
                    sum_s[pair, 0:1, :] = sum_s[pair, 0:1, :] * factor + jnp.sum(
                        weights, axis=0, keepdims=True
                    )
                    acc_s[pair] = acc_s[pair] * factor + dot(values, weights.astype(BF16), ((0,), (0,)))
                    m_s[pair, 0:1, :] = new

            if skip:
                pl.when((key_block <= query_block) & (key_block * BLK + BLK > first))(fold)
            else:
                fold()

        tiles = []
        for pair in range(KV_HEADS // 2):
            total = sum_s[pair, 0:1, :]
            lse_ref[qb, pair : pair + 1, :] = m_s[pair, 0:1, :] + jnp.log(total)
            acc = acc_s[pair] / total
            for i in range(2 * GROUP):
                head = pair * 2 * GROUP + i
                tile = jnp.transpose(acc[:, i * BLK : (i + 1) * BLK])
                if head % 2 != (head // GROUP) % 2:
                    tile = pltpu.roll(tile, HEAD, 1)
                tiles.append(tile)
                if head % 2 == 1:
                    both = jnp.where(lane_half(tile.shape, 0), tiles[head - 1], tile)
                    lanes = pl.ds((head // 2) * 128, 128)
                    exact_ref[rows, lanes] = both
                    out_ref[rows, lanes] = both.astype(BF16)


def attend_kernel(parts, lengths_ref, order_ref, mine_ref, *refs):
    attend_blocks(parts, True, lengths_ref, order_ref, mine_ref[0], *refs)


def attend(lengths, order, mine, projected, kv):
    rows = projected.shape[0]
    smem = pl.BlockSpec(memory_space=pltpu.SMEM)
    vmem = pl.BlockSpec(memory_space=pltpu.VMEM)
    wide = 2 * GROUP * BLK
    pairs = KV_HEADS // 2
    return pl.pallas_call(
        functools.partial(attend_kernel, lengths.shape[1]),
        out_shape=(
            jax.ShapeDtypeStruct((rows, HEADS * HEAD), F32),
            jax.ShapeDtypeStruct((rows, HEADS * HEAD), BF16),
            jax.ShapeDtypeStruct((rows // BLK, pairs, wide), F32),
        ),
        in_specs=[smem, smem, smem, vmem, vmem],
        out_specs=(vmem, vmem, vmem),
        scratch_shapes=[
            pltpu.VMEM((pairs, wide, 128), BF16),
            pltpu.VMEM((pairs, 8, wide), F32),
            pltpu.VMEM((pairs, 8, wide), F32),
            pltpu.VMEM((pairs, BLK, wide), F32),
        ],
        compiler_params=pltpu.CompilerParams(vmem_limit_bytes=48 * 2**20),
        cost_estimate=pl.CostEstimate(flops=10**10, bytes_accessed=10**7, transcendentals=10**7),
        name="attend",
    )(lengths, order, mine, projected, kv)


def attend_back_kernel(
    parts,
    lengths_ref,
    order_ref,
    mine_ref,
    q_ref,
    kv_ref,
    grad_ref,
    lse_ref,
    exact_ref,
    dq_ref,
    dkv_ref,
    q_s,
    g_s,
    delta_s,
    dq_s,
    dkv_s,
):
    width = KV_HEADS * HEAD

    @pl.loop(0, order_ref.shape[1])
    def _(kb):
        dkv_s[pl.ds(kb * BLK, BLK), :] = jnp.zeros((BLK, 2 * width), F32)

    for qb in range(q_ref.shape[0] // BLK):
        rows = pl.ds(qb * BLK, BLK)
        for pair in range(KV_HEADS // 2):
            q_s[pair] = head_tiles(q_ref, rows, pair, HEAD**-0.5)
            g_s[pair] = head_tiles(grad_ref, rows, pair, 1.0)
            dq_s[pair] = jnp.zeros((2 * GROUP * BLK, 128), F32)
            for i in range(2 * GROUP):
                head = pair * 2 * GROUP + i
                exact = exact_ref[rows, (head // 2) * 128 : (head // 2 + 1) * 128]
                if head % 2 != (head // GROUP) % 2:
                    exact = pltpu.roll(exact, HEAD, 1)
                product = exact * g_s[pair, i * BLK : (i + 1) * BLK, :].astype(F32)
                delta_s[pair : pair + 1, i * BLK : (i + 1) * BLK] = jnp.sum(
                    jnp.transpose(product), axis=0, keepdims=True
                )
        query_block = order_ref[0, mine_ref[0] + qb]
        first = first_row_start(lengths_ref, query_block, parts)

        @pl.loop(0, order_ref.shape[1])
        def _(kb):
            key_block = order_ref[0, kb]

            @pl.when((key_block <= query_block) & (key_block * BLK + BLK > first))
            def _():
                seen = block_visibility(lengths_ref, query_block, key_block, parts)
                key_rows = pl.ds(kb * BLK, BLK)
                for pair in range(KV_HEADS // 2):
                    key_lanes = pl.ds(pair * 128, 128)
                    value_lanes = pl.ds(width + pair * 128, 128)
                    keys = kv_ref[key_rows, key_lanes]
                    values = kv_ref[key_rows, value_lanes]
                    scores = dot(keys, q_s[pair], ((1,), (1,)))
                    scores = jnp.where(seen, scores, far_negative)
                    probs = jnp.exp(scores - lse_ref[qb, pair : pair + 1, :])
                    grad_probs = dot(values, g_s[pair], ((1,), (1,)))
                    grad_scores = (probs * (grad_probs - delta_s[pair : pair + 1, :])).astype(BF16)
                    dkv_s[key_rows, value_lanes] += dot(probs.astype(BF16), g_s[pair])
                    dkv_s[key_rows, key_lanes] += dot(grad_scores, q_s[pair])
                    dq_s[pair] += dot(grad_scores, keys, ((0,), (0,)))

        tiles = []
        for pair in range(KV_HEADS // 2):
            for i in range(2 * GROUP):
                head = pair * 2 * GROUP + i
                tile = dq_s[pair, i * BLK : (i + 1) * BLK, :] * HEAD**-0.5
                if head % 2 != (head // GROUP) % 2:
                    tile = pltpu.roll(tile, HEAD, 1)
                tiles.append(tile)
                if head % 2 == 1:
                    both = jnp.where(lane_half(tile.shape, 0), tiles[head - 1], tile)
                    dq_ref[rows, (head // 2) * 128 : (head // 2 + 1) * 128] = both.astype(BF16)

    @pl.loop(0, order_ref.shape[1])
    def _(kb):
        key_rows = pl.ds(kb * BLK, BLK)
        dkv_ref[key_rows, :] = dkv_s[key_rows, :].astype(BF16)


def attend_back(lengths, order, mine, projected, kv, grad_attended, lse, exact):
    rows = projected.shape[0]
    smem = pl.BlockSpec(memory_space=pltpu.SMEM)
    vmem = pl.BlockSpec(memory_space=pltpu.VMEM)
    wide = 2 * GROUP * BLK
    pairs = KV_HEADS // 2
    return pl.pallas_call(
        functools.partial(attend_back_kernel, lengths.shape[1]),
        out_shape=(
            jax.ShapeDtypeStruct((rows, HEADS * HEAD), BF16),
            jax.ShapeDtypeStruct(kv.shape, BF16),
        ),
        in_specs=[smem, smem, smem, vmem, vmem, vmem, vmem, vmem],
        out_specs=(vmem, vmem),
        scratch_shapes=[
            pltpu.VMEM((pairs, wide, 128), BF16),
            pltpu.VMEM((pairs, wide, 128), BF16),
            pltpu.VMEM((pairs, wide), F32),
            pltpu.VMEM((pairs, wide, 128), F32),
            pltpu.VMEM(kv.shape, F32),
        ],
        compiler_params=pltpu.CompilerParams(vmem_limit_bytes=56 * 2**20),
        cost_estimate=pl.CostEstimate(flops=10**9, bytes_accessed=10**6, transcendentals=10**5),
        name="attend_back",
    )(lengths, order, mine, projected, kv, grad_attended, lse, exact)


MESH = pl.DeviceIdType.MESH


def place(z, core, exp):
    return {"le": z, "rep": 0, "core": core, "exp": exp}


def x_of(exp):
    return (exp // 2) * 2 + 1 - exp % 2


def y_of(exp):
    return (1 - exp // 2) * 2 + exp % 2


def remote(src, dst, send_sem, recv_sem, device):
    return pltpu.make_async_remote_copy(
        src_ref=src,
        dst_ref=dst,
        send_sem=send_sem,
        recv_sem=recv_sem,
        device_id=device,
        device_id_type=MESH,
    )


def near_to_far(z):
    first_half = z < 2
    return [z, z + 1 - 2 * (z % 2), jnp.where(first_half, 3, 0), jnp.where(first_half, 2, 1)]


def between(z, zz):
    return ((z == 1) & (zz == 2)) | ((z == 2) & (zz == 1))


def meet(devices):
    barrier = pltpu.get_barrier_semaphore()
    for device in devices:
        pl.semaphore_signal(barrier, inc=1, device_id=device, device_id_type=MESH)
    pl.semaphore_wait(barrier, len(devices))


def front_kernel(
    layers,
    shard_ref,
    in_ref,
    down_ref,
    tokens_ref,
    lengths_ref,
    order_ref,
    target_ref,
    cotangent_ref,
    w_all_ref,
    w_in_ref,
    w_down_ref,
    first_ref,
    projected_ref,
    kv_ref,
    exact_ref,
    attended_ref,
    lse_ref,
    middle_ref,
    second_ref,
    gates_ref,
    slot_gates_ref,
    rows_ref,
    got_grads_ref,
    hot_s,
    grads_s,
    weights,
    kv_s,
    q_s,
    m_s,
    sum_s,
    acc_s,
    in_wide,
    down_wide,
    in_half,
    down_half,
    unit_sem,
    line_sem,
    x_sem,
    y_sem,
    far_sem,
    core_sem,
    half_sem,
    half_send,
    over_sem,
    over_send,
    kv_sem,
    kv_send,
    own_sem,
    wide_sem,
    grad_sem,
    grad_send,
):
    z, core, exp = lax.axis_index("le"), lax.axis_index("core"), lax.axis_index("exp")
    other = 1 - core
    x, y = x_of(exp), y_of(exp)
    ctx = z * 2 + core
    rows = shard_ref.shape[0]
    own_layer, mate, farthest, middle = near_to_far(z)
    order = [mate, middle, farthest, own_layer]
    wides = ((in_ref, in_wide), (down_ref, down_wide))
    halves = ((in_half, w_in_ref), (down_half, w_down_ref))

    loads = []
    for k, zz in enumerate(order):
        for a in range(2):
            load = pltpu.make_async_copy(wides[a][0].at[zz], wides[a][1].at[zz], wide_sem.at[a, k])
            load.start()
            loads.append(load)
    peers = [
        (zz, (exp + t) % 4)
        for s, zz in enumerate(order)
        for t in range(4)
        if not (s == layers - 1 and t == 0)
    ]
    meet([place(zz, core, ee) for zz, ee in peers] + [place(zz, other, exp) for zz in order])

    def number(zz, cc, ee):
        return (zz * 2 + cc) * 4 + ee

    def unit(zz, cc, ee):
        return weights.at[pl.ds(pl.multiple_of(number(zz, cc, ee) * rows, 16), rows), :]

    def send(src, who, sem, device):
        return remote(src, unit(*who), sem, unit_sem.at[number(*who)], device)

    def arrive(who):
        send(unit(*who), who, line_sem.at[0], place(z, other, exp)).wait_recv()

    started = []

    def go(copy, condition=None):
        if condition is None:
            copy.start()
        else:
            pl.when(condition)(copy.start)
        started.append((copy, condition))

    me = (z, core, exp)
    keep = pltpu.make_async_copy(shard_ref, unit(*me), own_sem.at[0])
    keep.start()
    go(send(shard_ref, me, line_sem.at[layers], place(z + 1, core, exp)), z < layers - 1)
    go(send(shard_ref, me, line_sem.at[layers + 1], place(z - 1, core, exp)), z > 0)
    go(send(shard_ref, me, x_sem.at[layers], place(z, core, x)))
    go(send(shard_ref, me, y_sem.at[layers], place(z, core, y)))
    go(send(shard_ref, me, core_sem.at[layers], place(z, other, exp)))

    slab = 16
    for k, zz in enumerate(order):
        for a in range(2):
            loads[2 * k + a].wait()
            src, dst = wides[a][1], halves[a][0]

            @pl.loop(0, src.shape[1] // slab)
            def _(i, zz=zz, src=src, dst=dst):
                at = pl.ds(pl.multiple_of(i * slab, slab), slab)
                dst[zz, at, :] = src[zz, at, :].astype(BF16)

    def half(a, source, p):
        src, dst = halves[a]
        n, cols = src.shape[1], src.shape[2] // 2
        return dst.at[pl.ds(source * n, n), pl.ds(pl.multiple_of(p * cols, 128), cols)]

    def mine(a, zz, p):
        src = halves[a][0]
        cols = src.shape[2] // 2
        return src.at[zz, :, pl.ds(pl.multiple_of(p * cols, 128), cols)]

    def layer(k):
        return jnp.where(z < layers // 2, k, layers - 1 - k)

    def ahead(zz):
        return between(z, zz)

    def hand_out(a, early):
        for s, zz in enumerate(order):
            across = ahead(zz)
            for p in range(2):
                if s == layers - 1 and p == 0:
                    continue
                pp = (core + p) % 2
                copy = remote(
                    mine(a, zz, pp),
                    half(a, ctx, pp),
                    half_send.at[a, s * 2 + p],
                    half_sem.at[a, ctx],
                    place(zz, pp, exp),
                )
                if early:
                    pl.when(across)(copy.start)
                else:
                    pl.when(~across)(copy.start)
                    started.append((copy, None))
        if not early:
            go(
                remote(
                    mine(a, z, core),
                    half(a, ctx, core),
                    over_send.at[a, 2 * layers],
                    over_sem.at[a, ctx],
                    place(z, other, exp),
                )
            )

    for k in range(layers):
        zz = layer(k)
        who = (zz, core, exp)

        @pl.when(zz != z)
        def _(who=who):
            arrive(who)

        go(send(unit(*who), who, line_sem.at[k], place(z + 1, core, exp)), (zz < z) & (z < layers - 1))
        go(send(unit(*who), who, line_sem.at[k], place(z - 1, core, exp)), (zz > z) & (z > 0))
        go(send(unit(*who), who, x_sem.at[k], place(z, core, x)), zz != z)
        go(send(unit(*who), who, y_sem.at[k], place(z, core, y)), zz != z)
        go(send(unit(*who), who, core_sem.at[k], place(z, other, exp)), zz != z)
        if k == 0:
            hand_out(0, True)

    def spread_rows(values, out):
        tile, cap = 256, out.shape[1]

        @pl.loop(0, values.shape[1] // tile)
        def _(i):
            at = pl.ds(pl.multiple_of(i * tile, tile), tile)
            spread_out = dot(hot_s[...], values[:, at]).astype(BF16)
            for e in range(out.shape[0]):
                out[e, :, at] = spread_out[e * cap : (e + 1) * cap]

    slot = lax.broadcasted_iota(jnp.int32, hot_s.shape, 0)
    takes = [slot == target_ref[k : k + 1, :] for k in range(2)]
    hot_s[...] = jnp.where(takes[0] | takes[1], 1.0, 0.0).astype(BF16)
    spread_rows(cotangent_ref, grads_s)

    for a in range(2):
        pltpu.make_async_copy(mine(a, z, core), half(a, ctx, core), own_sem.at[1 + a]).start()

    hand_out(0, False)

    for k in range(layers):
        zz = layer(k)
        from_x, from_y = (zz, core, x), (zz, core, y)
        arrive(from_x)
        go(send(unit(*from_x), from_x, core_sem.at[layers + 1 + k], place(z, other, exp)))
        if k % 2 == 0:
            go(send(unit(*from_x), from_x, far_sem.at[k], place(z, core, y)))
        arrive(from_y)
        go(send(unit(*from_y), from_y, core_sem.at[2 * layers + 1 + k], place(z, other, exp)))
        if k % 2 == 1:
            go(send(unit(*from_y), from_y, far_sem.at[k], place(z, core, x)))
    for k in range(layers):
        far = (layer(k), core, y_of(x))
        arrive(far)
        go(send(unit(*far), far, core_sem.at[3 * layers + 1 + k], place(z, other, exp)))
    for ee in range(4):
        for zz in range(layers):
            arrive((zz, other, ee))
    keep.wait()
    save = pltpu.make_async_copy(weights, w_all_ref, own_sem.at[3])
    save.start()

    depth, count = tokens_ref.shape[1], tokens_ref.shape[0]
    qkv_cols, head_cols = projected_ref.shape[1], HEADS * HEAD
    inputs = tokens_ref[...].astype(F32)
    gains = jnp.concatenate(
        [
            jnp.transpose(weights[i * 128 : (i + 1) * 128, qkv_cols : qkv_cols + AUX].astype(F32))[0:8, :]
            for i in range(depth // 128)
        ],
        axis=1,
    )
    first_ref[...] = (inputs * norm_scale(inputs) * gains[0:1, :]).astype(BF16)
    tile = 512

    @pl.loop(0, (qkv_cols - head_cols) // tile)
    def _(i):
        at = pl.ds(pl.multiple_of(head_cols + i * tile, tile), tile)
        projected_ref[:, at] = dot(first_ref[...], weights[:, at]).astype(BF16)

    def block(source):
        return kv_s.at[pl.ds(pl.multiple_of(source * count, 16), count), :]

    def share(src, source, sem, device):
        return remote(src, block(source), sem, kv_sem.at[source], device)

    own = projected_ref.at[:, pl.ds(head_cols, qkv_cols - head_cols)]
    keep_kv = pltpu.make_async_copy(own, block(ctx), own_sem.at[0])
    keep_kv.start()
    go(share(own, ctx, kv_send.at[2 * layers], place(z + 1, core, exp)), z < layers - 1)
    go(share(own, ctx, kv_send.at[2 * layers + 1], place(z - 1, core, exp)), z > 0)
    go(share(own, ctx, kv_send.at[2 * layers + 2], place(z, other, exp)))

    @pl.loop(0, head_cols // tile)
    def _(i):
        at = pl.ds(pl.multiple_of(i * tile, tile), tile)
        projected_ref[:, at] = dot(first_ref[...], weights[:, at]).astype(BF16)

    for k in range(layers):
        zz = layer(k)
        source = zz * 2 + core

        @pl.when(zz != z)
        def _(source=source):
            share(block(source), source, kv_send.at[0], place(z, other, exp)).wait_recv()

        go(share(block(source), source, kv_send.at[k], place(z + 1, core, exp)), (zz < z) & (z < layers - 1))
        go(share(block(source), source, kv_send.at[k], place(z - 1, core, exp)), (zz > z) & (z > 0))
        go(share(block(source), source, kv_send.at[layers + k], place(z, other, exp)), zz != z)

    hand_out(1, True)
    hand_out(1, False)

    me_slot = exp * layers + z
    keep_grads = pltpu.make_async_copy(grads_s.at[me_slot], got_grads_ref.at[me_slot], own_sem.at[4])
    keep_grads.start()
    for k, (zz, ee) in enumerate(peers):
        there = ee * layers + zz
        go(
            remote(
                grads_s.at[there],
                got_grads_ref.at[me_slot],
                grad_send.at[k],
                grad_sem.at[me_slot],
                place(zz, core, ee),
            )
        )

    def pass_over(a):
        for s, zz in enumerate(order[::-1]):
            for p in range(2):
                if s == 0 and p == 0:
                    continue
                source = zz * 2 + (core + p) % 2
                remote(
                    half(a, source, core),
                    half(a, source, core),
                    half_send.at[a, 0],
                    half_sem.at[a, source],
                    place(z, other, exp),
                ).wait_recv()
                go(
                    remote(
                        half(a, source, core),
                        half(a, source, core),
                        over_send.at[a, s * 2 + p],
                        over_sem.at[a, source],
                        place(z, other, exp),
                    )
                )

    pass_over(0)
    for zz in range(layers):
        source = zz * 2 + other
        share(block(source), source, kv_send.at[0], place(z, other, exp)).wait_recv()
    keep_kv.wait()
    save_kv = pltpu.make_async_copy(kv_s, kv_ref, own_sem.at[0])
    save_kv.start()

    attend_blocks(
        lengths_ref.shape[1],
        False,
        lengths_ref,
        order_ref,
        ctx * (count // BLK),
        projected_ref,
        kv_s,
        exact_ref,
        attended_ref,
        lse_ref,
        q_s,
        m_s,
        sum_s,
        acc_s,
    )
    tile = 256

    @pl.loop(0, depth // tile)
    def _(i):
        at = pl.ds(pl.multiple_of(i * tile, tile), tile)
        w_at = pl.ds(pl.multiple_of(qkv_cols + AUX + i * tile, 128), tile)
        middle_ref[:, at] = tokens_ref[:, at].astype(F32) + dot(attended_ref[...], weights[:, w_at])

    middle = middle_ref[...]
    second_ref[...] = (middle * norm_scale(middle) * gains[1:2, :]).astype(BF16)
    logits = dot(second_ref[...], weights[:, qkv_cols : qkv_cols + AUX])
    lane = lax.broadcasted_iota(jnp.int32, logits.shape, 1)
    token = lax.broadcasted_iota(jnp.int32, (count, count), 0)
    eye = token == lax.broadcasted_iota(jnp.int32, (count, count), 1)
    chosen = []
    for k in range(2):
        line = target_ref[2 + k : 3 + k, :].astype(F32)
        expert = jnp.sum(jnp.where(eye, line, 0.0), axis=1, keepdims=True)
        chosen.append(jnp.sum(jnp.where(lane.astype(F32) == expert + 2.0, logits, 0.0), axis=1, keepdims=True))
    largest = jnp.maximum(chosen[0], chosen[1])
    exps = [jnp.exp(value - largest) for value in chosen]
    total = exps[0] + exps[1]
    gates = [value / total for value in exps]
    gates_ref[...] = jnp.where(lane == 0, gates[0], jnp.where(lane == 1, gates[1], 0.0))
    spread_rows(second_ref, rows_ref)
    slot = lax.broadcasted_iota(jnp.int32, hot_s.shape, 0)
    by_slot = jnp.zeros(hot_s.shape, F32)
    for k in range(2):
        line = jnp.sum(jnp.where(eye, gates[k], 0.0), axis=0, keepdims=True)
        by_slot = by_slot + jnp.where(slot == target_ref[k : k + 1, :], line, 0.0)
    by_slot = jnp.sum(by_slot, axis=1, keepdims=True)
    cap = rows_ref.shape[1]
    eye = lax.broadcasted_iota(jnp.int32, (cap, 128), 0) == lax.broadcasted_iota(jnp.int32, (cap, 128), 1)
    for e in range(rows_ref.shape[0]):
        line = jnp.sum(jnp.where(eye, by_slot[e * cap : (e + 1) * cap], 0.0), axis=0, keepdims=True)
        slot_gates_ref[e] = jnp.broadcast_to(line, (8, 128))

    pass_over(1)
    for source in range(2 * layers):
        for a in range(2):
            remote(
                half(a, source, other),
                half(a, source, other),
                half_send.at[a, 0],
                over_sem.at[a, source],
                place(z, other, exp),
            ).wait_recv()
    for zz, ee in peers:
        source = ee * layers + zz
        remote(
            got_grads_ref.at[source],
            got_grads_ref.at[source],
            grad_send.at[0],
            grad_sem.at[source],
            place(zz, core, ee),
        ).wait_recv()
    keep_grads.wait()
    save_kv.wait()
    save.wait()
    for a in range(2):
        pltpu.make_async_copy(mine(a, z, core), half(a, ctx, core), own_sem.at[1 + a]).wait()
    for copy, condition in started:
        if condition is None:
            copy.wait_send()
        else:
            pl.when(condition)(copy.wait_send)


def front(shard, expert_in, expert_out, tokens, lengths, block_order, target, cotangent, qkv_cols):
    layers = expert_in.shape[0]
    rows_in, rows_out = expert_in.shape[1], expert_out.shape[1]
    depth, cols = shard.shape[0] * 8 * layers, shard.shape[1]
    count = tokens.shape[0]
    kv_shape = (count * 2 * layers, qkv_cols - HEADS * HEAD)
    wide, pairs = 2 * GROUP * BLK, KV_HEADS // 2
    slots = (EXPERTS, CAP, depth)
    any_space = pl.BlockSpec(memory_space=pl.ANY)
    smem = pl.BlockSpec(memory_space=pltpu.SMEM)
    vmem = pl.BlockSpec(memory_space=pltpu.VMEM)
    dma = pltpu.SemaphoreType.DMA
    return pl.pallas_call(
        functools.partial(front_kernel, layers),
        out_shape=(
            jax.ShapeDtypeStruct((depth, cols), BF16),
            jax.ShapeDtypeStruct((rows_in * 2 * layers, expert_in.shape[2]), BF16),
            jax.ShapeDtypeStruct((rows_out * 2 * layers, expert_out.shape[2]), BF16),
            jax.ShapeDtypeStruct((count, depth), BF16),
            jax.ShapeDtypeStruct((count, qkv_cols), BF16),
            jax.ShapeDtypeStruct(kv_shape, BF16),
            jax.ShapeDtypeStruct((count, HEADS * HEAD), F32),
            jax.ShapeDtypeStruct((count, HEADS * HEAD), BF16),
            jax.ShapeDtypeStruct((count // BLK, pairs, wide), F32),
            jax.ShapeDtypeStruct((count, depth), F32),
            jax.ShapeDtypeStruct((count, depth), BF16),
            jax.ShapeDtypeStruct((count, AUX), F32),
            jax.ShapeDtypeStruct((EXPERTS, 8, 128), F32),
            jax.ShapeDtypeStruct(slots, BF16),
            jax.ShapeDtypeStruct(slots, BF16),
        ),
        in_specs=[any_space] * 3 + [vmem, smem, smem, vmem, vmem],
        out_specs=(any_space,) * 3 + (vmem, vmem, any_space) + (vmem,) * 8 + (any_space,),
        scratch_shapes=[
            pltpu.VMEM((EXPERTS * CAP, count), BF16),
            pltpu.VMEM(slots, BF16),
            pltpu.VMEM((depth, cols), BF16),
            pltpu.VMEM(kv_shape, BF16),
            pltpu.VMEM((pairs, wide, 128), BF16),
            pltpu.VMEM((pairs, 8, wide), F32),
            pltpu.VMEM((pairs, 8, wide), F32),
            pltpu.VMEM((pairs, BLK, wide), F32),
            pltpu.VMEM(expert_in.shape, F32),
            pltpu.VMEM(expert_out.shape, F32),
            pltpu.VMEM(expert_in.shape, BF16),
            pltpu.VMEM(expert_out.shape, BF16),
            dma((8 * layers,)),
            dma((layers + 2,)),
            dma((layers + 1,)),
            dma((layers + 1,)),
            dma((layers,)),
            dma((4 * layers + 1,)),
            dma((2, 2 * layers)),
            dma((2, 2 * layers)),
            dma((2, 2 * layers)),
            dma((2, 2 * layers + 1)),
            dma((2 * layers,)),
            dma((2 * layers + 3,)),
            dma((5,)),
            dma((2, layers)),
            dma((4 * layers,)),
            dma((4 * layers,)),
        ],
        compiler_params=pltpu.CompilerParams(
            collective_id=0, has_side_effects=True, vmem_limit_bytes=60 * 2**20
        ),
        name="front",
    )(shard, expert_in, expert_out, tokens, lengths, block_order, target, cotangent)


def experts_kernel(
    layers,
    rows_ref,
    gates_ref,
    grads_ref,
    w_in_ref,
    w_down_ref,
    out_ref,
    back_ref,
    back_gates_ref,
    d_in_ref,
    d_down_ref,
    w_in,
    w_down,
    got,
    got_gates,
    x_s,
    grad_s,
    hidden_s,
    inner_s,
    back_s,
    back_gates_s,
    other_in,
    other_down,
    pair_in,
    pair_down,
    row_sem,
    row_send,
    gate_sem,
    gate_send,
    back_sem,
    back_send,
    back_gate_sem,
    back_gate_send,
    pair_sem,
    pair_send,
    load_sem,
):
    z, core, exp = lax.axis_index("le"), lax.axis_index("core"), lax.axis_index("exp")
    other = 1 - core
    columns = rows_ref.shape[0] // layers
    me = exp * layers + z
    cap, depth = rows_ref.shape[1], rows_ref.shape[2]
    chunk = columns * cap
    loads = [
        pltpu.make_async_copy(w_in_ref, w_in, load_sem.at[0]),
        pltpu.make_async_copy(w_down_ref, w_down, load_sem.at[1]),
    ]
    for load in loads:
        load.start()
    own_layer, mate, farthest, middle = near_to_far(z)
    peers = [
        (zz, (exp + t) % columns)
        for s, zz in enumerate([mate, farthest, middle, own_layer])
        for t in range(columns)
        if not (s == layers - 1 and t == 0)
    ]
    meet([place(zz, core, ee) for zz, ee in peers] + [place(z, other, exp)])

    started = []

    def go(copy):
        copy.start()
        started.append(copy)

    keeps = [
        pltpu.make_async_copy(rows_ref.at[me], got.at[me], load_sem.at[2]),
        pltpu.make_async_copy(gates_ref.at[me], got_gates.at[me], load_sem.at[3]),
    ]
    for keep in keeps:
        keep.start()
    for k, (zz, ee) in enumerate(peers):
        there = ee * layers + zz
        go(remote(gates_ref.at[there], got_gates.at[me], gate_send.at[k], gate_sem.at[me], place(zz, core, ee)))
        go(remote(rows_ref.at[there], got.at[me], row_send.at[k], row_sem.at[me], place(zz, core, ee)))
    for load in loads + keeps:
        load.wait()

    eye = lax.broadcasted_iota(jnp.int32, (cap, 128), 0) == lax.broadcasted_iota(jnp.int32, (cap, 128), 1)
    tile = 256

    def tiles(i):
        return pl.ds(pl.multiple_of(i * tile, tile), tile)

    for k, zz in enumerate([own_layer, mate, farthest, middle]):
        rows = pl.ds(k * chunk, chunk)
        for ee in range(columns):
            source = ee * layers + zz

            @pl.when(source != me)
            def _(source=source):
                here = place(z, other, exp)
                remote(got.at[source], got.at[source], row_send.at[0], row_sem.at[source], here).wait_recv()
                remote(
                    got_gates.at[source], got_gates.at[source], gate_send.at[0], gate_sem.at[source], here
                ).wait_recv()

            at = pl.ds(k * chunk + ee * cap, cap)
            x_s[at, :] = got[source]
            gate = jnp.sum(jnp.where(eye, got_gates[source, 0:1, :], 0.0), axis=1, keepdims=True)
            grad_s[at, :] = (gate * grads_ref[source].astype(F32)).astype(BF16)

        @pl.loop(0, FF // tile)
        def _(i, rows=rows):
            up_at = pl.ds(pl.multiple_of(FF + i * tile, tile), tile)
            gate = dot(x_s[rows, :], w_in[:, tiles(i)])
            up = dot(x_s[rows, :], w_in[:, up_at])
            grad_hidden = dot(grad_s[rows, :], w_down[tiles(i), :], ((1,), (1,)))
            sigmoid = jax.nn.sigmoid(gate)
            silu = gate * sigmoid
            hidden_s[rows, tiles(i)] = (silu * up).astype(BF16)
            inner_s[rows, tiles(i)] = (grad_hidden * up * sigmoid * (1.0 + gate * (1.0 - sigmoid))).astype(BF16)
            inner_s[rows, up_at] = (grad_hidden * silu).astype(BF16)

        @pl.loop(0, depth // tile)
        def _(i, rows=rows, zz=zz):
            back = dot(inner_s[rows, :], w_in[tiles(i), :], ((1,), (1,))).astype(BF16)
            for ee in range(columns):
                back_s[ee * layers + zz, :, tiles(i)] = back[ee * cap : (ee + 1) * cap]

        @pl.loop(0, depth // tile, init_carry=jnp.zeros((chunk, 128), F32))
        def gate_grads(i, sums, rows=rows, zz=zz):
            result = dot(hidden_s[rows, :], w_down[:, tiles(i)]).astype(BF16)
            parts = []
            for ee in range(columns):
                part = result[ee * cap : (ee + 1) * cap]
                out_ref[ee * layers + zz, :, tiles(i)] = part
                parts.append(part.astype(F32) * grads_ref[ee * layers + zz, :, tiles(i)].astype(F32))
            product = jnp.concatenate(parts, axis=0)
            return sums + product[:, :128] + product[:, 128:]

        gate_grads = jnp.sum(gate_grads, axis=1, keepdims=True)
        for ee in range(columns):
            there = ee * layers + zz
            column = gate_grads[ee * cap : (ee + 1) * cap]
            line = jnp.sum(jnp.where(eye, column, 0.0), axis=0, keepdims=True)
            back_gates_s[there] = jnp.broadcast_to(line, (8, 128))
            row_copy = remote(
                back_s.at[there],
                back_ref.at[me],
                back_send.at[there],
                back_sem.at[me],
                place(zz, core, ee),
            )
            gate_copy = remote(
                back_gates_s.at[there],
                back_gates_ref.at[me],
                back_gate_send.at[there],
                back_gate_sem.at[me],
                place(zz, core, ee),
            )

            @pl.when(there != me)
            def _(row_copy=row_copy, gate_copy=gate_copy):
                row_copy.start()
                gate_copy.start()

    own = [
        pltpu.make_async_copy(back_s.at[me], back_ref.at[me], load_sem.at[2]),
        pltpu.make_async_copy(back_gates_s.at[me], back_gates_ref.at[me], load_sem.at[3]),
    ]
    for copy in own:
        copy.start()

    half_in, half_down = d_in_ref.shape[1], d_down_ref.shape[1]

    def in_part(i, p):
        cols = pl.ds(pl.multiple_of(p * half_in, 128), half_in)
        return dot(x_s[:, tiles(i)], inner_s[:, cols], ((0,), (0,)))

    def down_part(i, p):
        cols = pl.ds(pl.multiple_of(p * half_down, 128), half_down)
        return dot(hidden_s[:, tiles(i)], grad_s[:, cols], ((0,), (0,)))

    @pl.loop(0, depth // tile)
    def _(i):
        other_in[tiles(i), :] = in_part(i, other).astype(BF16)

    go(remote(other_in, pair_in, pair_send.at[0], pair_sem.at[0], place(z, other, exp)))

    @pl.loop(0, FF // tile)
    def _(i):
        other_down[tiles(i), :] = down_part(i, other).astype(BF16)

    go(remote(other_down, pair_down, pair_send.at[1], pair_sem.at[1], place(z, other, exp)))
    remote(other_in, pair_in, pair_send.at[0], pair_sem.at[0], place(z, other, exp)).wait_recv()

    @pl.loop(0, depth // tile)
    def _(i):
        d_in_ref[tiles(i), :] = (in_part(i, core) + pair_in[tiles(i), :].astype(F32)).astype(BF16)

    remote(other_down, pair_down, pair_send.at[1], pair_sem.at[1], place(z, other, exp)).wait_recv()

    @pl.loop(0, FF // tile)
    def _(i):
        d_down_ref[tiles(i), :] = (down_part(i, core) + pair_down[tiles(i), :].astype(F32)).astype(BF16)

    for copy in own:
        copy.wait()
    for k, (zz, ee) in enumerate(peers):
        there = ee * layers + zz
        row_copy = remote(
            back_s.at[there], back_ref.at[there], back_send.at[there], back_sem.at[there], place(zz, core, ee)
        )
        gate_copy = remote(
            back_gates_s.at[there],
            back_gates_ref.at[there],
            back_gate_send.at[there],
            back_gate_sem.at[there],
            place(zz, core, ee),
        )
        row_copy.wait()
        gate_copy.wait()
    for copy in started:
        copy.wait_send()


def experts(rows, gates, grads, w_in, w_down, layers):
    count, cap, depth = rows.shape
    any_space = pl.BlockSpec(memory_space=pl.ANY)
    vmem = pl.BlockSpec(memory_space=pltpu.VMEM)
    dma = pltpu.SemaphoreType.DMA
    half_in = jax.ShapeDtypeStruct((depth, FF), BF16)
    half_down = jax.ShapeDtypeStruct((FF, depth // 2), BF16)
    return pl.pallas_call(
        functools.partial(experts_kernel, layers),
        out_shape=(
            jax.ShapeDtypeStruct(rows.shape, BF16),
            jax.ShapeDtypeStruct(rows.shape, BF16),
            jax.ShapeDtypeStruct(gates.shape, F32),
            half_in,
            half_down,
        ),
        in_specs=[any_space, any_space, vmem, any_space, any_space],
        out_specs=(vmem, any_space, any_space, vmem, vmem),
        scratch_shapes=[
            pltpu.VMEM(w_in.shape, BF16),
            pltpu.VMEM(w_down.shape, BF16),
            pltpu.VMEM(rows.shape, BF16),
            pltpu.VMEM(gates.shape, F32),
            pltpu.VMEM((count * cap, depth), BF16),
            pltpu.VMEM((count * cap, depth), BF16),
            pltpu.VMEM((count * cap, FF), BF16),
            pltpu.VMEM((count * cap, 2 * FF), BF16),
            pltpu.VMEM(rows.shape, BF16),
            pltpu.VMEM(gates.shape, F32),
            pltpu.VMEM(half_in.shape, BF16),
            pltpu.VMEM(half_down.shape, BF16),
            pltpu.VMEM(half_in.shape, BF16),
            pltpu.VMEM(half_down.shape, BF16),
        ]
        + [dma((count,))] * 8
        + [dma((2,)), dma((2,)), dma((4,))],
        compiler_params=pltpu.CompilerParams(
            collective_id=2, has_side_effects=True, vmem_limit_bytes=60 * 2**20
        ),
        name="experts",
    )(rows, gates, grads, w_in, w_down)


def add_rows(total, part, rows):
    slab = 16

    @pl.loop(0, rows // slab)
    def _(i):
        at = pl.ds(pl.multiple_of(i * slab, slab), slab)
        total[at, :] = (total[at, :].astype(F32) + part[at, :].astype(F32)).astype(BF16)


class Chain:
    def __init__(self, layers, z, above, below, own, rows, up, down, sems, sends):
        self.layers, self.z, self.above, self.below = layers, z, above, below
        self.own, self.rows, self.up, self.down = own, rows, up, down
        self.sems, self.sends = sems, sends
        self.parts = sems.shape[2]
        self.width = up.shape[2] // self.parts

    def columns(self, ref, h):
        return ref.at[:, pl.ds(h * self.width, self.width)]

    def rise(self, d, h):
        return remote(
            self.columns(self.own(d), h),
            self.columns(self.up.at[d], h),
            self.sends.at[0, d, h],
            self.sems.at[0, d, h],
            self.above,
        )

    def fall(self, d, h):
        return remote(
            self.columns(self.own(d), h),
            self.columns(self.down.at[d], h),
            self.sends.at[1, d, h],
            self.sems.at[1, d, h],
            self.below,
        )

    def end(self, step):
        for h in range(self.parts):
            pl.when(self.z == 0)(self.rise(self.layers - 1 - step, h).start)
            pl.when(self.z == self.layers - 1)(self.fall(step, h).start)

    def ends(self):
        for step in range(self.layers - 1):
            self.end(step)

    def add(self, d, h, buffer):
        add_rows(self.columns(self.own(d), h), self.columns(buffer.at[d], h), self.rows)

    def middle(self):
        z, last = self.z, self.layers - 1

        def pass_on(make, d, buffer):
            for h in range(self.parts):
                copy = make(d, h)
                copy.wait_recv()
                self.add(d, h, buffer)
                copy.start()

        def both(first_half):
            for step in range(last):
                high, low = last - step, step

                def upward(high=high):
                    pl.when((z > 0) & (z < high))(lambda: pass_on(self.rise, high, self.up))

                def downward(low=low):
                    pl.when((z < last) & (z > low))(lambda: pass_on(self.fall, low, self.down))

                for turn in (upward, downward) if first_half else (downward, upward):
                    turn()

        pl.when(z <= last // 2)(lambda: both(True))
        pl.when(z > last // 2)(lambda: both(False))

    def finish(self):
        z, last = self.z, self.layers - 1

        def take(make, buffer):
            for h in range(self.parts):
                make(z, h).wait_recv()
                self.add(z, h, buffer)

        pl.when(z > 0)(lambda: take(self.rise, self.up))
        pl.when(z < last)(lambda: take(self.fall, self.down))

    def wait_sends(self):
        for d in range(self.layers):
            for h in range(self.parts):
                pl.when(self.z < d)(self.rise(d, h).wait_send)
                pl.when(self.z > d)(self.fall(d, h).wait_send)


def finish_kernel(
    layers,
    grad_kv_ref,
    grad_q_ref,
    first_ref,
    tokens_ref,
    gain_ref,
    middle_ref,
    w_all_ref,
    attended_ref,
    second_ref,
    logits_ref,
    gain_moe_ref,
    base_ref,
    returned_ref,
    picks_ref,
    gates_ref,
    in_ref,
    down_ref,
    block_ref,
    d_tokens_ref,
    d_qkv_ref,
    d_out_ref,
    d_aux_ref,
    got_in_ref,
    got_down_ref,
    weights,
    projected,
    grad_first,
    kv_own,
    kv_pair,
    kv_up,
    kv_down,
    late_both,
    late_pair,
    late_near,
    late_up,
    late_down,
    q_both,
    q_pair,
    q_near,
    q_up,
    q_down,
    k_both,
    k_pair,
    k_near,
    k_up,
    k_down,
    load_sem,
    kv_pair_sem,
    kv_pair_send,
    kv_sem,
    kv_send,
    half_sem,
    half_send,
    pair_sem,
    pair_send,
    near_sem,
    near_send,
    line_sem,
    line_send,
):
    z, core, exp = lax.axis_index("le"), lax.axis_index("core"), lax.axis_index("exp")
    other = 1 - core
    partner = place(z, other, exp)
    above, below = place(z + 1, core, exp), place(z - 1, core, exp)
    x, y = x_of(exp), y_of(exp)
    mates = (x, y, y_of(x))
    own_layer, mate, farthest, middle = near_to_far(z)
    ctx = z * 2 + core
    rows = d_qkv_ref.shape[0]
    count = tokens_ref.shape[0]
    head_cols = HEADS * HEAD
    qkv_cols = d_qkv_ref.shape[1]
    kv_cols = qkv_cols - head_cols

    loads = []

    def load(src, dst):
        copy = pltpu.make_async_copy(src, dst, load_sem.at[len(loads)])
        copy.start()
        loads.append(copy)
        return copy

    kv_loads = [
        load(grad_kv_ref.at[pl.ds(pl.multiple_of((d * 2 + core) * count, 16), count), :], kv_own.at[d])
        for d in range(layers)
    ]
    depth = w_all_ref.shape[0]

    def weights_part(i):
        part = w_all_ref.at[pl.ds(i * depth // 2, depth // 2), pl.ds(0, qkv_cols)]
        return pltpu.make_async_copy(part, weights, load_sem.at[2 * layers + 2])

    weights_part(0).start()
    meet(
        [
            place((z + s) % layers, (core + p) % 2, exp)
            for s in range(layers)
            for p in range(2)
            if s + p > 0
        ]
        + [place(z, core, mate) for mate in mates]
    )
    started = []

    def go(copy):
        copy.start()
        started.append(copy)

    arrays = ((in_ref, got_in_ref), (down_ref, got_down_ref))

    def mine(a, owner):
        n = arrays[a][1].shape[1]
        return arrays[a][0].at[pl.ds(owner * n, n), :]

    def half(a, expert, p):
        cols = arrays[a][0].shape[1]
        return arrays[a][1].at[expert, :, pl.ds(pl.multiple_of(p * cols, 128), cols)]

    for a in range(2):
        load(mine(a, ctx), half(a, z, core))

    def hand_back(a, early):
        for s, zz in enumerate([mate, farthest, middle, own_layer]):
            across = between(z, zz)
            for p in range(2):
                if s == layers - 1 and p == 0:
                    continue
                pp = (core + p) % 2
                copy = remote(
                    mine(a, zz * 2 + pp),
                    half(a, z, core),
                    half_send.at[a, s * 2 + p],
                    half_sem.at[a, ctx],
                    place(zz, pp, exp),
                )
                if early:
                    pl.when(across)(copy.start)
                else:
                    pl.when(~across)(copy.start)
                    started.append(copy)

    hand_back(0, True)

    for d in range(layers):
        go(
            remote(
                grad_kv_ref.at[pl.ds(pl.multiple_of((d * 2 + other) * count, 16), count), :],
                kv_pair.at[d],
                kv_pair_send.at[d],
                kv_pair_sem.at[d],
                partner,
            )
        )
    kv_line = Chain(
        layers, z, above, below, lambda d: kv_own.at[d], count, kv_up, kv_down, kv_sem, kv_send
    )
    for copy in kv_loads:
        copy.wait()
    for k in range(layers):
        d = jnp.where(z < layers // 2, layers - 1 - k, k)
        remote(kv_pair.at[d], kv_pair.at[d], kv_pair_send.at[d], kv_pair_sem.at[d], partner).wait_recv()
        add_rows(kv_own.at[d], kv_pair.at[d], count)
        if k < layers - 1:
            kv_line.end(k)

    def near_copy(i, near, own, d, m, target):
        return remote(
            own.at[d, pl.ds(pl.multiple_of(target * rows, 16), rows), :],
            near.at[m, d],
            near_send.at[i, m, d],
            near_sem.at[i, m, d],
            place(z, core, mates[m]),
        )

    def pair_sums(i, own, pair, near):
        for d in range(layers):
            remote(pair.at[d], pair.at[d], pair_send.at[i, d], pair_sem.at[i, d], partner).wait_recv()
            add_rows(own.at[d], pair.at[d], 4 * rows)
            for m in range(3):
                go(near_copy(i, near, own, d, m, mates[m]))

    def near_sums(i, own, near):
        for d in range(layers):
            for m in range(3):
                near_copy(i, near, own, d, m, exp).wait_recv()
            mine = own.at[d, pl.ds(pl.multiple_of(exp * rows, 16), rows), :]

            @pl.loop(0, rows // 16)
            def _(r, mine=mine, d=d):
                at = pl.ds(pl.multiple_of(r * 16, 16), 16)
                total = mine[at, :].astype(F32)
                for m in range(3):
                    total = total + near[m, d, at, :].astype(F32)
                mine[at, :] = total.astype(BF16)

    def line_of(i, own, up, down):
        return Chain(
            layers,
            z,
            above,
            below,
            lambda d: own.at[d, pl.ds(pl.multiple_of(exp * rows, 16), rows), :],
            rows,
            up,
            down,
            line_sem.at[i],
            line_send.at[i],
        )

    def outer_product(both, cols, left, right, gains=None):
        for d in range(layers):
            block = left[:, d * 8 * rows : (d + 1) * 8 * rows]
            part = dot(block, right, ((0,), (0,)))
            if gains is not None:
                turned = [
                    jnp.transpose(jnp.broadcast_to(gains[:, at : at + 128], (128, 128)))
                    for at in range(d * 8 * rows, (d + 1) * 8 * rows, 128)
                ]
                lane = lax.broadcasted_iota(jnp.int32, part.shape, 1)
                part = jnp.where(lane == 0, jnp.concatenate(turned, axis=0), part)
            part = part.astype(BF16)
            both[0, d, :, cols] = part[: 4 * rows]
            both[1, d, :, cols] = part[4 * rows :]

    def pair_up(i, both, pair):
        for d in range(layers):
            go(remote(both.at[other, d], pair.at[d], pair_send.at[i, d], pair_sem.at[i, d], partner))

    outer_product(q_both, slice(0, head_cols), first_ref, grad_q_ref[...])
    pair_up(1, q_both, q_pair)
    width = middle_ref.shape[1]
    outer_product(late_both, slice(0, width), attended_ref, middle_ref[...].astype(BF16))
    outer_product(late_both, slice(width, width + AUX), second_ref, logits_ref[...], gain_moe_ref[...])
    pair_up(0, late_both, late_pair)
    late_own = late_both.at[core]
    q_own = q_both.at[core]
    pair_sums(1, q_own, q_pair, q_near)
    pair_sums(0, late_own, late_pair, late_near)
    kv_line.middle()
    hand_back(0, False)
    hand_back(1, True)
    hand_back(1, False)
    kv_line.finish()

    projected[:, :head_cols] = grad_q_ref[...]
    projected[:, head_cols:] = kv_own[z]
    outer_product(k_both, slice(0, kv_cols), first_ref, projected[:, head_cols:])
    tile = 256
    for i in range(2):
        weights_part(i).wait()

        @pl.loop(0, depth // 2 // tile)
        def _(j, i=i):
            at = pl.ds(pl.multiple_of(j * tile, tile), tile)
            to = pl.ds(pl.multiple_of(i * depth // 2 + j * tile, tile), tile)
            grad_first[:, to] = dot(projected[...], weights[at, :], ((1,), (1,)))

        if i == 0:
            weights_part(1).start()

    inputs = tokens_ref[...].astype(F32)
    scale = norm_scale(inputs)
    norm = inputs * scale
    grad = grad_first[...]
    grad_gain = jnp.sum(grad * norm, axis=0, keepdims=True)
    for d in range(layers):
        block = jnp.concatenate(
            [
                jnp.transpose(jnp.broadcast_to(grad_gain[:, at : at + 128], (128, 128)))
                for at in range(d * 8 * rows, (d + 1) * 8 * rows, 128)
            ],
            axis=0,
        ).astype(BF16)
        k_both[0, d, :, kv_cols:] = block[: 4 * rows]
        k_both[1, d, :, kv_cols:] = block[4 * rows :]
    pair_up(2, k_both, k_pair)
    grad = grad * gain_ref[...]
    d_tokens_ref[...] = (
        middle_ref[...] + scale * (grad - norm * jnp.mean(grad * norm, axis=-1, keepdims=True))
    ).astype(BF16)
    k_own = k_both.at[core]
    pair_sums(2, k_own, k_pair, k_near)

    @pl.loop(0, depth // tile)
    def _(i):
        at = pl.ds(pl.multiple_of(i * tile, tile), tile)
        total = base_ref[:, at]
        for k in range(2):
            total = total + gates_ref[:, k : k + 1] * dot(picks_ref[k], returned_ref[:, at])
        block_ref[:, at] = total.astype(BF16)

    late_line = line_of(0, late_own, late_up, late_down)
    q_line = line_of(1, q_own, q_up, q_down)
    k_line = line_of(2, k_own, k_up, k_down)
    near_sums(1, q_own, q_near)
    q_line.ends()
    near_sums(0, late_own, late_near)
    late_line.ends()
    q_line.middle()
    near_sums(2, k_own, k_near)
    k_line.ends()
    late_line.middle()
    k_line.middle()
    mine_rows = pl.ds(pl.multiple_of(exp * rows, 16), rows)
    q_line.finish()
    d_qkv_ref[:, :head_cols] = q_both[core, z, mine_rows, :].astype(F32)
    late_line.finish()
    last = late_both[core, z, mine_rows, :].astype(F32)
    d_out_ref[...] = last[:, :width]
    d_aux_ref[:, AUX:] = last[:, width:]
    k_line.finish()
    last = k_both[core, z, mine_rows, :].astype(F32)
    d_qkv_ref[:, head_cols:] = last[:, :kv_cols]
    d_aux_ref[:, :AUX] = last[:, kv_cols:]

    for source in range(2 * layers):
        for a in range(2):

            @pl.when(source != ctx)
            def _(source=source, a=a):
                remote(
                    half(a, source // 2, source % 2),
                    half(a, source // 2, source % 2),
                    half_send.at[a, 0],
                    half_sem.at[a, source],
                    partner,
                ).wait_recv()

    for copy in loads[-2:]:
        copy.wait()
    for line in (kv_line, late_line, q_line, k_line):
        line.wait_sends()
    for copy in started:
        copy.wait_send()


def finish(
    grad_kv,
    grad_q,
    first,
    tokens,
    gain,
    middle,
    w_all,
    attended,
    second,
    grad_logits,
    gain_moe,
    base,
    returned,
    picks,
    gates,
    grad_in,
    grad_down,
    layers,
):
    depth, count = first.shape[1], first.shape[0]
    rows = depth // (8 * layers)
    qkv_cols = grad_q.shape[1] + grad_kv.shape[1]
    n_in, n_down = grad_in.shape[0] // (2 * layers), grad_down.shape[0] // (2 * layers)
    any_space = pl.BlockSpec(memory_space=pl.ANY)
    vmem = pl.BlockSpec(memory_space=pltpu.VMEM)
    dma = pltpu.SemaphoreType.DMA

    def sums(cols):
        return [
            pltpu.VMEM((2, layers, 4 * rows, cols), BF16),
            pltpu.VMEM((layers, 4 * rows, cols), BF16),
            pltpu.VMEM((3, layers, rows, cols), BF16),
            pltpu.VMEM((layers, rows, cols), BF16),
            pltpu.VMEM((layers, rows, cols), BF16),
        ]

    return pl.pallas_call(
        functools.partial(finish_kernel, layers),
        out_shape=(
            jax.ShapeDtypeStruct((count, depth), BF16),
            jax.ShapeDtypeStruct((count, depth), BF16),
            jax.ShapeDtypeStruct((rows, qkv_cols), F32),
            jax.ShapeDtypeStruct((rows, depth), F32),
            jax.ShapeDtypeStruct((rows, 2 * AUX), F32),
            jax.ShapeDtypeStruct((layers, n_in, 2 * grad_in.shape[1]), BF16),
            jax.ShapeDtypeStruct((layers, n_down, 2 * grad_down.shape[1]), BF16),
        ),
        in_specs=[any_space] + [vmem] * 5 + [any_space] + [vmem] * 8 + [any_space] * 2,
        out_specs=(vmem,) * 5 + (any_space,) * 2,
        scratch_shapes=[
            pltpu.VMEM((depth // 2, qkv_cols), BF16),
            pltpu.VMEM((count, qkv_cols), BF16),
            pltpu.VMEM((count, depth), F32),
        ]
        + [pltpu.VMEM((layers, count, grad_kv.shape[1]), BF16)] * 4
        + sums(depth + AUX)
        + sums(grad_q.shape[1])
        + sums(grad_kv.shape[1] + AUX)
        + [
            dma((2 * layers + 3,)),
            dma((layers,)),
            dma((layers,)),
            dma((2, layers, 2)),
            dma((2, layers, 2)),
            dma((2, 2 * layers)),
            dma((2, 2 * layers)),
            dma((3, layers)),
            dma((3, layers)),
            dma((3, 3, layers)),
            dma((3, 3, layers)),
            dma((3, 2, layers, 1)),
            dma((3, 2, layers, 1)),
        ],
        compiler_params=pltpu.CompilerParams(
            collective_id=1, has_side_effects=True, vmem_limit_bytes=60 * 2**20
        ),
        name="finish",
    )(
        grad_kv,
        grad_q,
        first,
        tokens,
        gain,
        middle,
        w_all,
        attended,
        second,
        grad_logits,
        gain_moe,
        base,
        returned,
        picks,
        gates,
        grad_in,
        grad_down,
    )


def settle_kernel(count, aux_ref, *refs):
    for src, dst in zip(refs[:count], refs[count : 2 * count]):
        dst[...] = src[...].astype(dst.dtype)
    rows = aux_ref.shape[0]
    eye = lax.broadcasted_iota(jnp.int32, (rows, 128), 0) == lax.broadcasted_iota(jnp.int32, (rows, 128), 1)
    for at, dst in zip((0, AUX), refs[2 * count :]):
        line = jnp.sum(jnp.where(eye, aux_ref[:, at : at + 1], 0.0), axis=0, keepdims=True)
        dst[...] = line[:, :rows]
    block = jnp.concatenate([aux_ref[:, AUX:], jnp.zeros((128 - rows, AUX), F32)], axis=0)
    refs[-1][...] = jnp.transpose(block)[1 : 1 + EXPERTS, :rows]


def settle(aux, arrays, steps):
    def spec(array):
        if array.ndim == 2 and array.shape[0] % (16 * steps) == 0:
            return pl.BlockSpec((array.shape[0] // steps, array.shape[1]), lambda i: (i, 0))
        if array.ndim == 3 and array.shape[1] % (16 * steps) == 0:
            return pl.BlockSpec(
                (array.shape[0], array.shape[1] // steps, array.shape[2]), lambda i: (0, i, 0)
            )
        return pl.BlockSpec(array.shape, lambda i: (0,) * array.ndim)

    specs = [spec(array) for array, _ in arrays]
    rows = aux.shape[0]
    small = [jax.ShapeDtypeStruct(shape, F32) for shape in ((1, rows), (1, rows), (EXPERTS, rows))]
    return pl.pallas_call(
        functools.partial(settle_kernel, len(arrays)),
        grid=(steps,),
        out_shape=[jax.ShapeDtypeStruct(array.shape, dtype) for array, dtype in arrays] + small,
        in_specs=[spec(aux)] + specs,
        out_specs=specs + [spec(shape) for shape in small],
        compiler_params=pltpu.CompilerParams(vmem_limit_bytes=60 * 2**20),
        name="settle",
    )(aux, *[array for array, _ in arrays])


CTX = ("le", "rep", "core")
ALL = ("le", "rep", "core", "exp")
OWNERS = ("exp", "le")


def on_device(
    tokens,
    cotangent,
    routes,
    lengths,
    block_order,
    gain_attn,
    qkv_weight,
    out_weight,
    gain_moe,
    router_weight,
    expert_in,
    expert_out,
):
    tok_rows = tokens.shape[1]
    head_width = HEADS * HEAD
    exp_local = expert_in.shape[0]
    n_ctx = D // expert_in.shape[1]
    copies = n_ctx // exp_local
    n_exp = EXPERTS // exp_local
    in_rows, out_rows = expert_in.shape[1], expert_out.shape[1]

    route_hot = (
        routes[0][:, :, None] == jnp.arange(EXPERTS, dtype=jnp.int32)[None, None, :]
    ).astype(F32)
    flat_hot = route_hot.reshape(tok_rows * 2, EXPERTS).astype(BF16)
    order = jnp.arange(tok_rows * 2, dtype=jnp.int32)
    earlier = (order[:, None] > order[None, :]).astype(BF16)
    ranks = dot(earlier, flat_hot)
    slot_index = jnp.sum(ranks * flat_hot.astype(F32), axis=1).astype(jnp.int32)
    target = (routes[0].reshape(tok_rows * 2) * CAP + slot_index).reshape(tok_rows, 2)
    slots = jnp.arange(EXPERTS * CAP, dtype=jnp.int32)
    picks = [(target[:, k : k + 1] == slots[None, :]) for k in range(2)]
    sends = [(target[:, k][None, :] == slots[:, None]) for k in range(2)]
    send_hot = (sends[0] | sends[1]).astype(BF16)

    def to_experts(rows):
        return lax.all_to_all(
            rows.reshape((EXPERTS, CAP) + rows.shape[1:]),
            OWNERS,
            split_axis=0,
            concat_axis=0,
            tiled=True,
        ).reshape(rows.shape)

    cols = qkv_weight.shape[1]
    aux = jnp.concatenate([gain_attn[:, None], gain_moe[:, None], router_weight], axis=1)
    aux = jnp.pad(aux, ((0, 0), (0, AUX - aux.shape[1])))
    shard = jnp.concatenate([qkv_weight, aux, out_weight], axis=1).astype(BF16)
    special = (copies, exp_local, n_exp) == (2, 4, 4)
    if special:
        (
            w_all,
            w_in,
            w_down,
            first,
            projected,
            kv,
            exact,
            attended,
            lse,
            middle,
            second,
            gates,
            slot_gates,
            second_rows,
            grad_y_rows,
        ) = front(
            shard,
            expert_in,
            expert_out,
            tokens[0],
            lengths,
            block_order,
            jnp.concatenate([target, routes[0]], axis=1).T,
            cotangent[0],
            cols,
        )
        gates = gates[:, :2]
    else:
        w_all = lax.all_gather(shard, ALL, axis=0, tiled=True)

        def to_owner(weight):
            rows, width = weight.shape[1:]
            halves = weight.astype(BF16).reshape(exp_local, rows, 2, width // 2).transpose(0, 2, 1, 3)
            halves = jnp.broadcast_to(
                halves[:, None], (exp_local, copies // 2, 2, rows, width // 2)
            ).reshape(n_ctx, rows, width // 2)
            mine = lax.all_to_all(halves, CTX, split_axis=0, concat_axis=0, tiled=True)
            return lax.all_gather(mine.reshape(n_ctx * rows, width // 2), "core", axis=1, tiled=True)

        w_in = to_owner(expert_in)
        w_down = to_owner(expert_out)
    w_qkv = w_all[:, :cols]
    aux_all = w_all[:, cols : cols + AUX]
    w_attn_out = w_all[:, cols + AUX :]
    gain_first = aux_all[:, 0].astype(F32)
    gain_second = aux_all[:, 1].astype(F32)
    w_router = aux_all[:, 2 : 2 + EXPERTS]

    inputs = tokens[0].astype(F32)
    scale_first = norm_scale(inputs)
    norm_first = inputs * scale_first
    mine = (lax.axis_index(CTX) * (tok_rows // BLK)).astype(jnp.int32).reshape(1)
    if not special:
        first = (norm_first * gain_first).astype(BF16)
        projected = dot(first, w_qkv).astype(BF16)
        kv = lax.all_gather(projected[:, head_width:], CTX, axis=0, tiled=True)
        kv, grad_y_send = lax.optimization_barrier((kv, dot(send_hot, cotangent[0]).astype(BF16)))
        grad_y_rows = to_experts(grad_y_send)
        exact, attended, lse = attend(lengths, block_order, mine, projected, kv)
        middle = inputs + dot(attended, w_attn_out)
    scale_second = norm_scale(middle)
    norm_second = middle * scale_second
    if not special:
        second = (norm_second * gain_second).astype(BF16)
        logits = dot(second, w_router)
        chosen = jnp.sum(route_hot * logits[:, None, :], axis=-1)
        gates = jax.nn.softmax(chosen, axis=-1)

    if special:
        expert_rows, grad_returned, gate_grads, grad_in, grad_down = experts(
            second_rows,
            slot_gates,
            grad_y_rows,
            w_in,
            w_down,
            exp_local,
        )
        returned = to_experts(expert_rows.reshape(EXPERTS * CAP, D))
        grad_returned = grad_returned.reshape(EXPERTS * CAP, D)
        gate_grads = gate_grads[:, 0, :CAP].reshape(1, EXPERTS * CAP)
    else:
        gate_rows = jnp.sum(
            jnp.where(sends[0], gates[:, 0][None, :], 0.0) + jnp.where(sends[1], gates[:, 1][None, :], 0.0),
            axis=1,
            keepdims=True,
        )

        def in_parts(column):
            high = lax.reduce_precision(column, 8, 7)
            rest = column - high
            mid = lax.reduce_precision(rest, 8, 7)
            parts = jnp.concatenate([high, mid, rest - mid], axis=1).astype(BF16)
            return jnp.pad(parts, ((0, 0), (0, AUX - 3)))

        gate_parts = in_parts(gate_rows)
        payload = to_experts(
            jnp.concatenate([dot(send_hot, second).astype(BF16), gate_parts], axis=1)
        )
        received = payload[:, :D]
        gate_got = jnp.sum(payload[:, D : D + 3].astype(F32), axis=1, keepdims=True)

        gate_up = dot(received, w_in)
        gate_part = gate_up[:, :FF]
        up_part = gate_up[:, FF:]
        sigmoid_gate = jax.nn.sigmoid(gate_part)
        silu_gate = gate_part * sigmoid_gate
        hidden = (silu_gate * up_part).astype(BF16)
        expert_rows = dot(hidden, w_down)
        expert_rows = expert_rows.astype(BF16)
        grad_y_rows = grad_y_rows.astype(F32)
        returned = to_experts(expert_rows)

        grad_rows = (gate_got * grad_y_rows).astype(BF16)
        gate_grad_parts = in_parts(
            jnp.sum(grad_y_rows * expert_rows.astype(F32), axis=1, keepdims=True)
        )
        half_d = D // 2
        grad_hidden = dot(grad_rows, w_down, ((1,), (1,)))
        grad_gate = (
            grad_hidden * up_part * sigmoid_gate * (1.0 + gate_part * (1.0 - sigmoid_gate))
        ).astype(BF16)
        grad_up = (grad_hidden * silu_gate).astype(BF16)
        grad_gate_up = jnp.concatenate([grad_gate, grad_up], axis=1)
        grad_back = dot(grad_gate_up, w_in, ((1,), (1,)))
        grad_returned = to_experts(jnp.concatenate([grad_back.astype(BF16), gate_grad_parts], axis=1))

        grad_in = jnp.stack(
            [dot(received, grad_gate, ((0,), (0,))), dot(received, grad_up, ((0,), (0,)))]
        ).astype(BF16)
        grad_down = jnp.stack(
            [
                dot(hidden, grad_rows[:, :half_d], ((0,), (0,))),
                dot(hidden, grad_rows[:, half_d:], ((0,), (0,))),
            ]
        ).astype(BF16)

        grad_in = lax.psum_scatter(grad_in, "core", scatter_dimension=0, tiled=True)[0]
        grad_down = lax.psum_scatter(grad_down, "core", scatter_dimension=0, tiled=True)[0]
        grad_returned, grad_in, grad_down = lax.optimization_barrier((grad_returned, grad_in, grad_down))
        gate_grads = jnp.sum(grad_returned[:, D:].astype(F32), axis=1).reshape(1, EXPERTS * CAP)
        grad_returned = grad_returned[:, :D]

    grad_y = cotangent[0].astype(F32)
    pick_hot = [p.astype(BF16) for p in picks]
    grad_gates = jnp.concatenate(
        [jnp.sum(jnp.where(p, gate_grads, 0.0), axis=1, keepdims=True) for p in picks], axis=1
    )
    grad_chosen = gates * (grad_gates - jnp.sum(gates * grad_gates, axis=-1, keepdims=True))
    grad_logits = jnp.sum(grad_chosen[:, :, None] * route_hot, axis=1).astype(BF16)
    grad_second = dot(pick_hot[0] + pick_hot[1], grad_returned) + dot(
        grad_logits, w_router, ((1,), (1,))
    )
    grad_gain_second = jnp.sum(grad_second * norm_second, axis=0)
    grad_norm_second = grad_second * gain_second
    grad_middle = grad_y + scale_second * (
        grad_norm_second
        - norm_second * jnp.mean(grad_norm_second * norm_second, axis=-1, keepdims=True)
    )
    grad_branch = grad_middle.astype(BF16)
    grad_attended = dot(grad_branch, w_attn_out, ((1,), (1,))).astype(BF16)
    grad_queries, grad_kv = attend_back(
        lengths, block_order, mine, projected, kv, grad_attended, lse, exact
    )
    grad_queries, grad_kv, returned = lax.optimization_barrier((grad_queries, grad_kv, returned))
    if special:
        block_out, grad_inputs, sum_qkv, sum_out, sum_aux, sum_in, sum_down = finish(
            grad_kv,
            grad_queries,
            first,
            tokens[0],
            gain_first[None, :],
            grad_middle,
            w_all,
            attended,
            second,
            jnp.pad(grad_logits, ((0, 0), (1, AUX - 1 - EXPERTS))),
            grad_gain_second[None, :],
            middle,
            returned,
            jnp.stack(pick_hot),
            gates,
            grad_in,
            grad_down,
            exp_local,
        )
        block_out, grad_inputs, sum_qkv, sum_out, sum_in, sum_down, gain_a, gain_m, sum_router = settle(
            sum_aux,
            (
                (block_out, BF16),
                (grad_inputs, BF16),
                (sum_qkv, F32),
                (sum_out, F32),
                (sum_in, F32),
                (sum_down, F32),
            ),
            4,
        )
        gain_a, gain_m, sum_router = gain_a[0], gain_m[0], sum_router.T
    else:
        grad_router = dot(second, grad_logits, ((0,), (0,)))
        grad_attn_out = dot(attended, grad_branch, ((0,), (0,)))
        late = jnp.concatenate([grad_gain_second[:, None], grad_router], axis=1)
        late = jnp.pad(late, ((0, 0), (0, AUX - late.shape[1])))
        late = jnp.concatenate([grad_attn_out.astype(BF16), late.astype(BF16)], axis=1)
        grad_kv = lax.psum_scatter(grad_kv, CTX, scatter_dimension=0, tiled=True)
        grad_projected = jnp.concatenate([grad_queries, grad_kv], axis=1)
        grad_qkv = dot(first, grad_projected, ((0,), (0,)))
        grad_first = dot(grad_projected, w_qkv, ((1,), (1,)))
        grad_gain_first = jnp.sum(grad_first * norm_first, axis=0)
        grad_norm_first = grad_first * gain_first
        grad_inputs = grad_middle + scale_first * (
            grad_norm_first
            - norm_first * jnp.mean(grad_norm_first * norm_first, axis=-1, keepdims=True)
        )
        grad_inputs = grad_inputs.astype(BF16)
        last = jnp.pad(grad_gain_first[:, None], ((0, 0), (0, AUX - 1)))
        part = jnp.concatenate([grad_qkv.astype(BF16), last.astype(BF16), late], axis=1)
        total = lax.psum_scatter(part, ALL, scatter_dimension=0, tiled=True).astype(F32)
        sum_qkv, sum_out = total[:, :cols], total[:, cols + AUX : cols + AUX + D]
        gain_a, gain_m = total[:, cols], total[:, cols + AUX + D]
        sum_router = total[:, cols + AUX + D + 1 : cols + AUX + D + 1 + EXPERTS]
        picked = [dot(p, returned) for p in pick_hot]
        block_out = (middle + gates[:, 0:1] * picked[0] + gates[:, 1:2] * picked[1]).astype(BF16)

        def to_rows(half, rows):
            width = half.shape[1]
            got = lax.all_to_all(
                half.reshape(n_ctx, rows, width), CTX, split_axis=0, concat_axis=0, tiled=True
            ).astype(F32)
            got = got.reshape(exp_local, copies // 2, 2, rows, width).sum(axis=1)
            return got.transpose(0, 2, 1, 3).reshape(exp_local, rows, 2 * width)

        sum_in = to_rows(grad_in, in_rows)
        sum_down = to_rows(grad_down, out_rows)
    return (
        block_out[None],
        grad_inputs[None],
        gain_a,
        sum_qkv,
        sum_out,
        gain_m,
        sum_router,
        sum_in.astype(F32),
        sum_down.astype(F32),
    )


def solution(mesh):
    n_ctx, n_exp = mesh.shape["ctx"], mesh.shape["exp"]
    exp_local = EXPERTS // n_exp
    copies = n_ctx // exp_local
    inner = Mesh(mesh.devices.reshape(exp_local, copies // 2, 2, n_exp), ALL)
    by_token = P("exp", CTX, None)
    by_row = P(ALL, None)
    by_expert = P("exp", CTX, None)
    return jax.shard_map(
        on_device,
        mesh=inner,
        in_specs=(
            by_token,
            by_token,
            by_token,
            P("exp", None),
            P("exp", None),
            P(ALL),
            by_row,
            by_row,
            P(ALL),
            by_row,
            by_expert,
            by_expert,
        ),
        out_specs=(
            by_token,
            by_token,
            P(ALL),
            by_row,
            by_row,
            P(ALL),
            by_row,
            by_expert,
            by_expert,
        ),
        check_vma=False,
    )
```

profile of v0, /device:TPU:8, one launch (start us, length us, event | category | flops | bytes accessed | tf_op | source)
XLA Modules:
  0.0 553.3 jit_solution(3896438902388603065)
XLA Ops:
  0.7 0.8 copy.55
  1.6 0.1 eq.78
  1.7 0.3 fusion.5
  2.0 0.1 convert_element_type.82
  2.2 0.7 multiply_add_fusion.1
  2.9 1.1 convert.23
  4.3 0.6 add_bitcast_fusion.target_ref
  5.0 0.8 pad_maximum_fusion.shard_ref
  5.8 204.5 %front.1 = (bf16[1536,4224]{1,0:T(8,128)(2,1)}, bf16[1536,2048]{1,0:T(8,128)(2,1)}, bf16[1024,1536]{1,0:T(8,128)(2,1)}, bf16[256,1536]{1,0:T(8,128)(2,1)}, bf16[...) custom-call(bf16[48,4224]{1,0:T(8,128)(2,1)} %pad_maximum_fusion.sha, ...), custom_call_target="tpu_custom_call" | custom-call | tf_op jit(solution)/shard_map/front/pallas_call | solution.py:748
  210.3 116.1 %experts.1 = (bf16[16,48,1536]{2,1,0:T(8,128)(2,1)}, bf16[16,48,1536]{2,1,0:T(8,128)(2,1)}, f32[16,8,128]{2,1,0:T(8,128)}, bf16[1536,1024]{1,0:T(8,128)(2,1)}, bf16[1024,768]{1,0:T(8,128)(2,1)}) custom-call(bf16[16,48,1536]{2,1,0:T(8,128)(2,1)} %get-tuple-element.53.rows_ref, f32[16,8,128]{2,1,0:T(8,128)} %get-tuple-element.54.gates_ref, ...), custom_call_target="tpu_custom_call" | custom-call | tf_op jit(solution)/shard_map/experts/pallas_call | solution.py:1030
  326.4 7.9 %all-to-all-start = ((bf16[16,48,1536]{2,1,0:T(8,128)(2,1)}), bf16[16,48,1536]{2,1,0:T(8,128)(2,1)}, u32[]{:S(2)}, u32[]{:S(2)}) async-start(bf16[16,48,1536]{2,1,0:T(8,128)(2,1)} %get-tuple-element.66), calls=%async_computation | async-start | bytes 4718592 | tf_op jit(solution)/shard_map/all_to_all | solution.py:1675
  334.3 1.0 slice_reduce_fusion
  335.4 0.3 select_reduce_fusion.1
  335.7 0.1 copy.57
  335.9 0.7 fusion.22
  336.6 0.1 copy.58
  336.9 0.1 copy.60
  337.0 1.6 convert_reduce_fusion
  338.5 0.2 multiply_reduce_fusion.2
  338.7 2.5 fusion.10
  341.3 1.8 multiply_reduce_fusion
  343.1 0.6 broadcast_in_dim.59.gain_moe_ref
  343.7 0.7 pad.10.logits_ref
  344.4 0.6 reshape.155.gain_ref
  345.0 0.4 multiply_add_fusion.middle_ref
  345.5 5.2 fusion.2.grad_ref
  350.7 20.7 %attend_back.1 = (bf16[256,1536]{1,0:T(8,128)(2,1)}, bf16[2048,1024]{1,0:T(8,128)(2,1)}) custom-call(s32[1,3]{1,0:T(1,128)} %lengths_ref.3, s32[1,16]{1,0:T(1,128)} %order_ref.3, s32[1]{0:T(128)} %bitcast.mine_ref, bf16[256,2560]{1,0:T(8,128)(2,1)} %get-tuple-element.50.q_ref, bf16[2048,1024]{1,0:T(8,128)(2,1)} %get-tuple-element.51.kv_ref, ...), custom_call_target="tpu_custom_call" | custom-call | flops 1000000000 | bytes 1000000 | tf_op jit(solution)/shard_map/attend_back/pallas_call | solution.py:269
  371.4 0.3 iota_compare_fusion.2
  371.7 1.0 add_convert_fusion.picks_ref
  372.7 11.1 %all-to-all-done = bf16[16,48,1536]{2,1,0:T(8,128)(2,1)} async-done(((bf16[16,48,1536]{2,1,0:T(8,128)(2,1)}), bf16[16,48,1536]{2,1,0:T(8,128)(2,1)}, u32[]{:S(2)}, u32[]{:S(2)}) %all-to-all-start) | async-done | bytes 2359328 | tf_op jit(solution)/shard_map/all_to_all | solution.py:1675
  383.8 161.5 %finish.1 = (bf16[256,1536]{1,0:T(8,128)(2,1)}, bf16[256,1536]{1,0:T(8,128)(2,1)}, f32[48,2560]{1,0:T(8,128)}, f32[48,1536]{1,0:T(8,128)}, f32[48,256]{1,0:T(8,1...) custom-call(bf16[2048,1024]{1,0:T(8,128)(2,1)} %get-tuple-element.67.grad_kv_ref, ...), custom_call_target="tpu_custom_call" | custom-call | tf_op jit(solution)/shard_map/finish/pallas_call | solution.py:1535
  545.4 7.8 %settle.1 = (bf16[256,1536]{1,0:T(8,128)(2,1)}, bf16[256,1536]{1,0:T(8,128)(2,1)}, f32[48,2560]{1,0:T(8,128)}, f32[48,1536]{1,0:T(8,128)}, f32[4,192,2048]{2,1,0...) custom-call(f32[48,256]{1,0:T(8,128)} %get-tuple-element.75.aux_ref, ...), custom_call_target="tpu_custom_call" | custom-call | tf_op jit(solution)/shard_map/settle/pallas_call | solution.py:1622
  (37 shorter events, 0.8 us)
Async XLA Ops:
  0.6 3.7 copy-start.5
  0.7 3.3 copy-start.4
  0.7 3.3 copy-start.6
  0.7 3.4 copy-start.7
  0.7 3.5 copy-start.8
  326.4 9.5 %copy-start.3 = (f32[256,128]{1,0:T(8,128)S(1)}, f32[256,128]{1,0:T(8,128)}, u32[]{:S(2)}) copy-start(f32[256,128]{1,0:T(8,128)} %get-tuple-element.59) | copy-start | bytes 393220
  326.4 57.4 %all-to-all-start = ((bf16[16,48,1536]{2,1,0:T(8,128)(2,1)}), bf16[16,48,1536]{2,1,0:T(8,128)(2,1)}, u32[]{:S(2)}, u32[]{:S(2)}) async-start(bf16[16,48,1536]{2,1,0:T(8,128)(2,1)} %get-tuple-element.66), calls=%async_computation | async-start | bytes 4718592 | tf_op jit(solution)/shard_map/all_to_all | solution.py:1675
  334.3 4.2 copy-start
  341.3 3.8 copy-start.2
  345.5 5.2 copy-start.1
where the time goes:
time: 555 us; the launch traced here: 553 us
  Pallas kernels  511 us (92%)
  waiting for transfers between devices  11.1 us (2%)
  matrix products  9.82 us (2%)
  starting transfers between devices  7.9 us (1%)
  other arithmetic  7.76 us (1%)
    pallas_call x1, Pallas kernels, front(): pl.pallas_call(functools.partial(front_kernel, layers), out_shape=(jax.Sh...  205 us
    pallas_call x1, Pallas kernels, finish(): pl.pallas_call(functools.partial(finish_kernel, layers), out_shape=(jax.S...  162 us
    pallas_call x1, Pallas kernels, experts(): pl.pallas_call(functools.partial(experts_kernel, layers), out_shape=(jax....  116 us
    pallas_call x1, Pallas kernels, attend_back(): pl.pallas_call(functools.partial(attend_back_kernel, lengths.shape[1]), o...  20.7 us
    all_to_all x1, waiting for transfers between devices, to_experts(): lax.all_to_all(rows.reshape((EXPERTS, CAP) + rows.shape[1:]), OWNERS, spl...  11.1 us
  transfers between devices with their start and end apart: 1, of which 1 were waited for; matrix products, arithmetic and copies ran while one was open for 3% of the time, Pallas kernels for 4%

commit v1 on v0

--- a/solution.py
+++ b/solution.py
@@ -1170,13 +1170,8 @@
     second_ref,
     logits_ref,
     gain_moe_ref,
-    base_ref,
-    returned_ref,
-    picks_ref,
-    gates_ref,
     in_ref,
     down_ref,
-    block_ref,
     d_tokens_ref,
     d_qkv_ref,
     d_out_ref,
@@ -1442,14 +1437,6 @@
     k_own = k_both.at[core]
     pair_sums(2, k_own, k_pair, k_near)
 
-    @pl.loop(0, depth // tile)
-    def _(i):
-        at = pl.ds(pl.multiple_of(i * tile, tile), tile)
-        total = base_ref[:, at]
-        for k in range(2):
-            total = total + gates_ref[:, k : k + 1] * dot(picks_ref[k], returned_ref[:, at])
-        block_ref[:, at] = total.astype(BF16)
-
     late_line = line_of(0, late_own, late_up, late_down)
     q_line = line_of(1, q_own, q_up, q_down)
     k_line = line_of(2, k_own, k_up, k_down)
@@ -1507,10 +1494,6 @@
     second,
     grad_logits,
     gain_moe,
-    base,
-    returned,
-    picks,
-    gates,
     grad_in,
     grad_down,
     layers,
@@ -1536,15 +1519,14 @@
         functools.partial(finish_kernel, layers),
         out_shape=(
             jax.ShapeDtypeStruct((count, depth), BF16),
-            jax.ShapeDtypeStruct((count, depth), BF16),
             jax.ShapeDtypeStruct((rows, qkv_cols), F32),
             jax.ShapeDtypeStruct((rows, depth), F32),
             jax.ShapeDtypeStruct((rows, 2 * AUX), F32),
             jax.ShapeDtypeStruct((layers, n_in, 2 * grad_in.shape[1]), BF16),
             jax.ShapeDtypeStruct((layers, n_down, 2 * grad_down.shape[1]), BF16),
         ),
-        in_specs=[any_space] + [vmem] * 5 + [any_space] + [vmem] * 8 + [any_space] * 2,
-        out_specs=(vmem,) * 5 + (any_space,) * 2,
+        in_specs=[any_space] + [vmem] * 5 + [any_space] + [vmem] * 4 + [any_space] * 2,
+        out_specs=(vmem,) * 4 + (any_space,) * 2,
         scratch_shapes=[
             pltpu.VMEM((depth // 2, qkv_cols), BF16),
             pltpu.VMEM((count, qkv_cols), BF16),
@@ -1585,16 +1567,19 @@
         second,
         grad_logits,
         gain_moe,
-        base,
-        returned,
-        picks,
-        gates,
         grad_in,
         grad_down,
     )
 
 
-def settle_kernel(count, aux_ref, *refs):
+def settle_kernel(count, base_ref, gates_ref, target_ref, returned_ref, aux_ref, *refs):
+    block_ref, refs = refs[count], refs[:count] + refs[count + 1 :]
+    total = base_ref[...]
+    slot = lax.broadcasted_iota(jnp.int32, (total.shape[0], returned_ref.shape[0]), 1)
+    for k in range(2):
+        pick = jnp.where(target_ref[:, k : k + 1] == slot, 1.0, 0.0).astype(BF16)
+        total = total + gates_ref[:, k : k + 1] * dot(pick, returned_ref[...])
+    block_ref[...] = total.astype(BF16)
     for src, dst in zip(refs[:count], refs[count : 2 * count]):
         dst[...] = src[...].astype(dst.dtype)
     rows = aux_ref.shape[0]
@@ -1606,7 +1591,7 @@
     refs[-1][...] = jnp.transpose(block)[1 : 1 + EXPERTS, :rows]
 
 
-def settle(aux, arrays, steps):
+def settle(base, gates, target, returned, aux, arrays, steps):
     def spec(array):
         if array.ndim == 2 and array.shape[0] % (16 * steps) == 0:
             return pl.BlockSpec((array.shape[0] // steps, array.shape[1]), lambda i: (i, 0))
@@ -1622,12 +1607,21 @@
     return pl.pallas_call(
         functools.partial(settle_kernel, len(arrays)),
         grid=(steps,),
-        out_shape=[jax.ShapeDtypeStruct(array.shape, dtype) for array, dtype in arrays] + small,
-        in_specs=[spec(aux)] + specs,
-        out_specs=specs + [spec(shape) for shape in small],
+        out_shape=[jax.ShapeDtypeStruct(base.shape, BF16)]
+        + [jax.ShapeDtypeStruct(array.shape, dtype) for array, dtype in arrays]
+        + small,
+        in_specs=[
+            spec(base),
+            spec(gates),
+            spec(target),
+            pl.BlockSpec(returned.shape, lambda i: (0, 0)),
+            spec(aux),
+        ]
+        + specs,
+        out_specs=[spec(base)] + specs + [spec(shape) for shape in small],
         compiler_params=pltpu.CompilerParams(vmem_limit_bytes=60 * 2**20),
         name="settle",
-    )(aux, *[array for array, _ in arrays])
+    )(base, gates, target, returned, aux, *[array for array, _ in arrays])
 
 
 CTX = ("le", "rep", "core")
@@ -1850,9 +1844,8 @@
     grad_queries, grad_kv = attend_back(
         lengths, block_order, mine, projected, kv, grad_attended, lse, exact
     )
-    grad_queries, grad_kv, returned = lax.optimization_barrier((grad_queries, grad_kv, returned))
     if special:
-        block_out, grad_inputs, sum_qkv, sum_out, sum_aux, sum_in, sum_down = finish(
+        grad_inputs, sum_qkv, sum_out, sum_aux, sum_in, sum_down = finish(
             grad_kv,
             grad_queries,
             first,
@@ -1864,18 +1857,17 @@
             second,
             jnp.pad(grad_logits, ((0, 0), (1, AUX - 1 - EXPERTS))),
             grad_gain_second[None, :],
-            middle,
-            returned,
-            jnp.stack(pick_hot),
-            gates,
             grad_in,
             grad_down,
             exp_local,
         )
         block_out, grad_inputs, sum_qkv, sum_out, sum_in, sum_down, gain_a, gain_m, sum_router = settle(
+            middle,
+            gates,
+            target,
+            returned,
             sum_aux,
             (
-                (block_out, BF16),
                 (grad_inputs, BF16),
                 (sum_qkv, F32),
                 (sum_out, F32),

time: 555 us -> 547 us (0.986)
  waiting for transfers between devices: 11.1 us -> 0.01 us
  Pallas kernels: 511 us -> 519 us
    pallas_call x1, Pallas kernels: 162 us -> 174 us  [finish(): pl.pallas_call(functools.partial(finish_kernel, layers), out_shape=(jax.S...]
    all_to_all x1, waiting for transfers between devices: 11.1 us -> 0.01 us  [to_experts(): lax.all_to_all(rows.reshape((EXPERTS, CAP) + rows.shape[1:]), OWNERS, spl...]
    pallas_call x1, Pallas kernels: 20.7 us -> 13.5 us  [attend_back(): pl.pallas_call(functools.partial(attend_back_kernel, lengths.shape[1]), o...]
  transfers between devices with their start and end apart: 1 -> 1, of which waited for: 1 -> 0; matrix products, arithmetic and copies ran while one was open for 3% -> 3% of each run, Pallas kernels for 4% -> 34%
where the time goes in v1:
time: 547 us; the launch traced here: 546 us
  Pallas kernels  519 us (95%)
  matrix products  8.17 us (1%)
  starting transfers between devices  7.9 us (1%)
    pallas_call x1, Pallas kernels, front(): pl.pallas_call(functools.partial(front_kernel, layers), out_shape=(jax.Sh...  204 us
    pallas_call x1, Pallas kernels, finish(): pl.pallas_call(functools.partial(finish_kernel, layers), out_shape=(jax.S...  174 us
    pallas_call x1, Pallas kernels, experts(): pl.pallas_call(functools.partial(experts_kernel, layers), out_shape=(jax....  116 us
    pallas_call x1, Pallas kernels, attend_back(): pl.pallas_call(functools.partial(attend_back_kernel, lengths.shape[1]), o...  13.5 us
  transfers between devices with their start and end apart: 1, of which 0 were waited for; matrix products, arithmetic and copies ran while one was open for 3% of the time, Pallas kernels for 34%

profile of v1, /device:TPU:8, one launch (start us, length us, event | category | flops | bytes accessed | tf_op | source)
XLA Modules:
  0.0 546.1 jit_solution(11399457155821696848)
XLA Ops:
  0.7 0.9 copy.60
  1.6 0.1 eq.52
  1.7 0.3 fusion.5
  2.0 0.1 convert_element_type.68
  2.5 0.1 copy.59
  2.6 0.1 copy.57
  2.7 0.1 copy.58
  2.8 0.6 add_bitcast_fusion.target_ref
  3.5 0.8 pad_maximum_fusion.shard_ref
  4.2 204.5 %front.1 = (bf16[1536,4224]{1,0:T(8,128)(2,1)}, bf16[1536,2048]{1,0:T(8,128)(2,1)}, bf16[1024,1536]{1,0:T(8,128)(2,1)}, bf16[256,1536]{1,0:T(8,128)(2,1)}, bf16[...) custom-call(bf16[48,4224]{1,0:T(8,128)(2,1)} %pad_maximum_fusion.sha, ...), custom_call_target="tpu_custom_call" | custom-call | tf_op jit(solution)/shard_map/front/pallas_call | solution.py:748
  208.7 116.1 %experts.1 = (bf16[16,48,1536]{2,1,0:T(8,128)(2,1)}, bf16[16,48,1536]{2,1,0:T(8,128)(2,1)}, f32[16,8,128]{2,1,0:T(8,128)}, bf16[1536,1024]{1,0:T(8,128)(2,1)}, bf16[1024,768]{1,0:T(8,128)(2,1)}) custom-call(bf16[16,48,1536]{2,1,0:T(8,128)(2,1)} %get-tuple-element.48.rows_ref, f32[16,8,128]{2,1,0:T(8,128)} %get-tuple-element.49.gates_ref, ...), custom_call_target="tpu_custom_call" | custom-call | tf_op jit(solution)/shard_map/experts/pallas_call | solution.py:1030
  324.8 7.9 %all-to-all-start = ((bf16[16,48,1536]{2,1,0:T(8,128)(2,1)}), bf16[16,48,1536]{2,1,0:T(8,128)(2,1)}, u32[]{:S(2)}, u32[]{:S(2)}) async-start(bf16[16,48,1536]{2,1,0:T(8,128)(2,1)} %get-tuple-element.53), calls=%async_computation | async-start | bytes 4718592 | tf_op jit(solution)/shard_map/all_to_all | solution.py:1669
  332.7 1.0 slice_reduce_fusion.2
  333.8 0.2 slice_reduce_fusion.1
  334.0 0.3 select_reduce_fusion.1
  334.3 0.1 copy.65
  334.5 0.1 multiply_reduce_fusion.3
  334.6 0.1 copy.66
  334.8 0.7 slice_multiply_fusion
  335.5 0.1 copy.68
  335.7 1.7 convert_reduce_fusion
  337.4 0.2 multiply_reduce_fusion.2
  337.6 0.9 fusion.10
  338.5 1.8 multiply_reduce_fusion
  340.3 0.6 broadcast_in_dim.59.gain_moe_ref
  340.9 0.7 pad.10.logits_ref
  341.6 0.6 reshape.73.gain_ref
  342.3 0.5 multiply_add_fusion.middle_ref
  342.7 5.2 fusion.2.grad_ref
  347.9 13.5 %attend_back.1 = (bf16[256,1536]{1,0:T(8,128)(2,1)}, bf16[2048,1024]{1,0:T(8,128)(2,1)}) custom-call(s32[1,3]{1,0:T(1,128)} %lengths_ref.3, s32[1,16]{1,0:T(1,128)} %order_ref.3, s32[1]{0:T(128)} %bitcast.7.mine_ref, bf16[256,2560]{1,0:T(8,128)(2,1)} %get-tuple-element.54.q_ref, bf16[2048,1024]{1,0:T(8,128)(2,1)} %get-tuple-element.55.kv_ref, ...), custom_call_target="tpu_custom_call" | custom-call | flops 1000000000 | bytes 1000000 | tf_op jit(solution)/shard_map/attend_back/pallas_call | solution.py:269
  361.4 174.0 %finish.1 = (bf16[256,1536]{1,0:T(8,128)(2,1)}, f32[48,2560]{1,0:T(8,128)}, f32[48,1536]{1,0:T(8,128)}, f32[48,256]{1,0:T(8,128)}, bf16[4,192,2048]{2,1,0:T(8,128)(2,1)}, /*index=5*/bf16[4,128,1536]{2,1,0:T(8,128)(2,1)}) custom-call(bf16[2048,1024]{1,0:T(8,128)(2,1)} %get-tuple-element.61.grad_kv_ref, bf16[256,1536]{1,0:T(8,128)(2,1)} %get-tuple-element.62.grad_q_ref, ...), custom_call_target="tpu_custom_call" | custom-call | tf_op jit(solution)/shard_map/finish/pallas_call | solution.py:1518
  535.4 10.5 %settle.1 = (bf16[256,1536]{1,0:T(8,128)(2,1)}, bf16[256,1536]{1,0:T(8,128)(2,1)}, f32[48,2560]{1,0:T(8,128)}, f32[48,1536]{1,0:T(8,128)}, f32[4,192,2048]{2,1,0...) custom-call(f32[256,1536]{1,0:T(8,128)} %get-tuple-element.46.base_ref, ...), custom_call_target="tpu_custom_call" | custom-call | tf_op jit(solution)/shard_map/settle/pallas_call | solution.py:1607
  (40 shorter events, 0.6 us)
Async XLA Ops:
  0.6 1.7 copy-start.5
  0.7 1.7 copy-start.6
  0.7 1.8 copy-start.7
  0.7 1.9 copy-start.9
  0.7 2.0 copy-start.10
  2.2 331.6 %copy-start.2 = (s32[256,2]{1,0:T(8,128)}, s32[256,2]{1,0:T(8,128)S(1)}, u32[]{:S(2)}) copy-start(s32[256,2]{1,0:T(8,128)S(1)} %multiply_add_fusion.1.target_ref) | copy-start | bytes 6148
  324.8 9.7 %copy-start.4 = (f32[256,128]{1,0:T(8,128)S(1)}, f32[256,128]{1,0:T(8,128)}, u32[]{:S(2)}) copy-start(f32[256,128]{1,0:T(8,128)} %get-tuple-element.47) | copy-start | bytes 393220
  324.8 210.6 %all-to-all-start = ((bf16[16,48,1536]{2,1,0:T(8,128)(2,1)}), bf16[16,48,1536]{2,1,0:T(8,128)(2,1)}, u32[]{:S(2)}, u32[]{:S(2)}) async-start(bf16[16,48,1536]{2,1,0:T(8,128)(2,1)} %get-tuple-element.53), calls=%async_computation | async-start | bytes 4718592 | tf_op jit(solution)/shard_map/all_to_all | solution.py:1669
  332.7 4.7 copy-start
  335.7 1.9 copy-start.8
  338.5 3.8 copy-start.3
  342.7 5.2 copy-start.1

commit v2 on v1

--- a/solution.py
+++ b/solution.py
@@ -352,6 +352,7 @@
     second_ref,
     gates_ref,
     slot_gates_ref,
+    gains_ref,
     rows_ref,
     got_grads_ref,
     hot_s,
@@ -562,6 +563,7 @@
         ],
         axis=1,
     )
+    gains_ref[...] = gains
     first_ref[...] = (inputs * norm_scale(inputs) * gains[0:1, :]).astype(BF16)
     tile = 512
 
@@ -761,11 +763,12 @@
             jax.ShapeDtypeStruct((count, depth), BF16),
             jax.ShapeDtypeStruct((count, AUX), F32),
             jax.ShapeDtypeStruct((EXPERTS, 8, 128), F32),
+            jax.ShapeDtypeStruct((8, depth), F32),
             jax.ShapeDtypeStruct(slots, BF16),
             jax.ShapeDtypeStruct(slots, BF16),
         ),
         in_specs=[any_space] * 3 + [vmem, smem, smem, vmem, vmem],
-        out_specs=(any_space,) * 3 + (vmem, vmem, any_space) + (vmem,) * 8 + (any_space,),
+        out_specs=(any_space,) * 3 + (vmem, vmem, any_space) + (vmem,) * 9 + (any_space,),
         scratch_shapes=[
             pltpu.VMEM((EXPERTS * CAP, count), BF16),
             pltpu.VMEM(slots, BF16),
@@ -1430,7 +1433,7 @@
         k_both[0, d, :, kv_cols:] = block[: 4 * rows]
         k_both[1, d, :, kv_cols:] = block[4 * rows :]
     pair_up(2, k_both, k_pair)
-    grad = grad * gain_ref[...]
+    grad = grad * gain_ref[0:1, :]
     d_tokens_ref[...] = (
         middle_ref[...] + scale * (grad - norm * jnp.mean(grad * norm, axis=-1, keepdims=True))
     ).astype(BF16)
@@ -1540,8 +1543,8 @@
             dma((2 * layers + 3,)),
             dma((layers,)),
             dma((layers,)),
-            dma((2, layers, 2)),
-            dma((2, layers, 2)),
+            dma((2, layers, 4)),
+            dma((2, layers, 4)),
             dma((2, 2 * layers)),
             dma((2, 2 * layers)),
             dma((3, layers)),
@@ -1588,7 +1591,7 @@
         line = jnp.sum(jnp.where(eye, aux_ref[:, at : at + 1], 0.0), axis=0, keepdims=True)
         dst[...] = line[:, :rows]
     block = jnp.concatenate([aux_ref[:, AUX:], jnp.zeros((128 - rows, AUX), F32)], axis=0)
-    refs[-1][...] = jnp.transpose(block)[1 : 1 + EXPERTS, :rows]
+    refs[-1][...] = jnp.transpose(block)[2 : 2 + EXPERTS, :rows]
 
 
 def settle(base, gates, target, returned, aux, arrays, steps):
@@ -1694,6 +1697,7 @@
             second,
             gates,
             slot_gates,
+            gain_rows,
             second_rows,
             grad_y_rows,
         ) = front(
@@ -1726,7 +1730,7 @@
     aux_all = w_all[:, cols : cols + AUX]
     w_attn_out = w_all[:, cols + AUX :]
     gain_first = aux_all[:, 0].astype(F32)
-    gain_second = aux_all[:, 1].astype(F32)
+    gain_second = gain_rows[1] if special else aux_all[:, 1].astype(F32)
     w_router = aux_all[:, 2 : 2 + EXPERTS]
 
     inputs = tokens[0].astype(F32)
@@ -1829,11 +1833,13 @@
         [jnp.sum(jnp.where(p, gate_grads, 0.0), axis=1, keepdims=True) for p in picks], axis=1
     )
     grad_chosen = gates * (grad_gates - jnp.sum(gates * grad_gates, axis=-1, keepdims=True))
-    grad_logits = jnp.sum(grad_chosen[:, :, None] * route_hot, axis=1).astype(BF16)
+    lanes = jnp.arange(AUX, dtype=jnp.int32) - 2
+    wide_hot = (routes[0][:, :, None] == lanes[None, None, :]).astype(F32)
+    grad_logits = jnp.sum(grad_chosen[:, :, None] * wide_hot, axis=1).astype(BF16)
     grad_second = dot(pick_hot[0] + pick_hot[1], grad_returned) + dot(
-        grad_logits, w_router, ((1,), (1,))
+        grad_logits, aux_all, ((1,), (1,))
     )
-    grad_gain_second = jnp.sum(grad_second * norm_second, axis=0)
+    grad_gain_second = jnp.sum(grad_second * norm_second, axis=0, keepdims=True)
     grad_norm_second = grad_second * gain_second
     grad_middle = grad_y + scale_second * (
         grad_norm_second
@@ -1850,13 +1856,13 @@
             grad_queries,
             first,
             tokens[0],
-            gain_first[None, :],
+            gain_rows,
             grad_middle,
             w_all,
             attended,
             second,
-            jnp.pad(grad_logits, ((0, 0), (1, AUX - 1 - EXPERTS))),
-            grad_gain_second[None, :],
+            grad_logits,
+            grad_gain_second,
             grad_in,
             grad_down,
             exp_local,
@@ -1878,9 +1884,9 @@
         )
         gain_a, gain_m, sum_router = gain_a[0], gain_m[0], sum_router.T
     else:
-        grad_router = dot(second, grad_logits, ((0,), (0,)))
+        grad_router = dot(second, grad_logits[:, 2 : 2 + EXPERTS], ((0,), (0,)))
         grad_attn_out = dot(attended, grad_branch, ((0,), (0,)))
-        late = jnp.concatenate([grad_gain_second[:, None], grad_router], axis=1)
+        late = jnp.concatenate([grad_gain_second.T, grad_router], axis=1)
         late = jnp.pad(late, ((0, 0), (0, AUX - late.shape[1])))
         late = jnp.concatenate([grad_attn_out.astype(BF16), late.astype(BF16)], axis=1)
         grad_kv = lax.psum_scatter(grad_kv, CTX, scatter_dimension=0, tiled=True)

time: 547 us -> 546 us (level)
  no operation moved by 1% of the time
where the time goes in v2:
time: 546 us; the launch traced here: 544 us
  Pallas kernels  517 us (95%)
  matrix products  9.72 us (2%)
  starting transfers between devices  7.91 us (1%)
    pallas_call x1, Pallas kernels, front(): pl.pallas_call(functools.partial(front_kernel, layers), out_shape=(jax.Sh...  205 us
    pallas_call x1, Pallas kernels, finish(): pl.pallas_call(functools.partial(finish_kernel, layers), out_shape=(jax.S...  170 us
    pallas_call x1, Pallas kernels, experts(): pl.pallas_call(functools.partial(experts_kernel, layers), out_shape=(jax....  116 us
    pallas_call x1, Pallas kernels, attend_back(): pl.pallas_call(functools.partial(attend_back_kernel, lengths.shape[1]), o...  16.4 us
  transfers between devices with their start and end apart: 1, of which 0 were waited for; matrix products, arithmetic and copies ran while one was open for 3% of the time, Pallas kernels for 34%

profile of v2, /device:TPU:8, one launch (start us, length us, event | category | flops | bytes accessed | tf_op | source)
XLA Modules:
  0.0 544.3 jit_solution(2755416885954434985)
XLA Ops:
  0.7 0.9 copy.59
  1.6 0.1 eq.59
  1.7 0.3 fusion.5
  2.0 0.1 convert_element_type.44
  2.3 0.1 copy.62
  2.5 0.1 copy.58
  2.6 0.1 copy.56
  2.7 0.1 copy.57
  2.8 0.6 add_bitcast_fusion.target_ref
  3.4 0.1 fusion.21
  3.5 0.8 pad_maximum_fusion.shard_ref
  4.2 204.5 %front.1 = (bf16[1536,4224]{1,0:T(8,128)(2,1)}, bf16[1536,2048]{1,0:T(8,128)(2,1)}, bf16[1024,1536]{1,0:T(8,128)(2,1)}, bf16[256,1536]{1,0:T(8,128)(2,1)}, bf16[...) custom-call(bf16[48,4224]{1,0:T(8,128)(2,1)} %pad_maximum_fusion.sha, ...), custom_call_target="tpu_custom_call" | custom-call | tf_op jit(solution)/shard_map/front/pallas_call | solution.py:750
  208.8 116.0 %experts.1 = (bf16[16,48,1536]{2,1,0:T(8,128)(2,1)}, bf16[16,48,1536]{2,1,0:T(8,128)(2,1)}, f32[16,8,128]{2,1,0:T(8,128)}, bf16[1536,1024]{1,0:T(8,128)(2,1)}, bf16[1024,768]{1,0:T(8,128)(2,1)}) custom-call(bf16[16,48,1536]{2,1,0:T(8,128)(2,1)} %get-tuple-element.49.rows_ref, f32[16,8,128]{2,1,0:T(8,128)} %get-tuple-element.50.gates_ref, ...), custom_call_target="tpu_custom_call" | custom-call | tf_op jit(solution)/shard_map/experts/pallas_call | solution.py:1033
  324.8 7.9 %all-to-all-start = ((bf16[16,48,1536]{2,1,0:T(8,128)(2,1)}), bf16[16,48,1536]{2,1,0:T(8,128)(2,1)}, u32[]{:S(2)}, u32[]{:S(2)}) async-start(bf16[16,48,1536]{2,1,0:T(8,128)(2,1)} %get-tuple-element.54), calls=%async_computation | async-start | bytes 4718592 | tf_op jit(solution)/shard_map/all_to_all | solution.py:1672
  332.7 1.0 slice_reduce_fusion.2
  333.8 0.2 slice_reduce_fusion.1
  334.0 0.3 select_reduce_fusion.1
  334.4 0.1 copy.64
  334.5 0.1 multiply_reduce_fusion.3
  334.6 0.1 copy.65
  334.8 0.7 slice_multiply_fusion
  335.5 0.8 slice_reduce_fusion.3
  336.4 0.2 select_reduce_fusion.2.logits_ref
  336.6 0.2 multiply_reduce_fusion.2
  336.8 2.5 fusion.10
  339.3 1.7 multiply_reduce_fusion
  341.1 0.6 broadcast_in_dim.58.gain_moe_ref
  341.7 0.5 multiply_add_fusion.middle_ref
  342.2 5.2 fusion.2.grad_ref
  347.4 16.4 %attend_back.1 = (bf16[256,1536]{1,0:T(8,128)(2,1)}, bf16[2048,1024]{1,0:T(8,128)(2,1)}) custom-call(s32[1,3]{1,0:T(1,128)} %lengths_ref.3, s32[1,16]{1,0:T(1,128)} %order_ref.3, s32[1]{0:T(128)} %bitcast.7.mine_ref, bf16[256,2560]{1,0:T(8,128)(2,1)} %get-tuple-element.55.q_ref, bf16[2048,1024]{1,0:T(8,128)(2,1)} %get-tuple-element.56.kv_ref, ...), custom_call_target="tpu_custom_call" | custom-call | flops 1000000000 | bytes 1000000 | tf_op jit(solution)/shard_map/attend_back/pallas_call | solution.py:269
  363.8 169.8 %finish.1 = (bf16[256,1536]{1,0:T(8,128)(2,1)}, f32[48,2560]{1,0:T(8,128)}, f32[48,1536]{1,0:T(8,128)}, f32[48,256]{1,0:T(8,128)}, bf16[4,192,2048]{2,1,0:T(8,128)(2,1)}, /*index=5*/bf16[4,128,1536]{2,1,0:T(8,128)(2,1)}) custom-call(bf16[2048,1024]{1,0:T(8,128)(2,1)} %get-tuple-element.63.grad_kv_ref, bf16[256,1536]{1,0:T(8,128)(2,1)} %get-tuple-element.64.grad_q_ref, ...), custom_call_target="tpu_custom_call" | custom-call | tf_op jit(solution)/shard_map/finish/pallas_call | solution.py:1521
  533.6 10.5 %settle.1 = (bf16[256,1536]{1,0:T(8,128)(2,1)}, bf16[256,1536]{1,0:T(8,128)(2,1)}, f32[48,2560]{1,0:T(8,128)}, f32[48,1536]{1,0:T(8,128)}, f32[4,192,2048]{2,1,0...) custom-call(f32[256,1536]{1,0:T(8,128)} %get-tuple-element.47.base_ref, ...), custom_call_target="tpu_custom_call" | custom-call | tf_op jit(solution)/shard_map/settle/pallas_call | solution.py:1610
  (38 shorter events, 0.4 us)
Async XLA Ops:
  0.6 1.7 copy-start.6
  0.7 1.7 copy-start.7
  0.7 1.8 copy-start.8
  0.7 1.9 copy-start.9
  0.7 2.0 copy-start.10
  2.2 331.6 %copy-start.2 = (s32[256,2]{1,0:T(8,128)}, s32[256,2]{1,0:T(8,128)S(1)}, u32[]{:S(2)}) copy-start(s32[256,2]{1,0:T(8,128)S(1)} %multiply_add_fusion.1.target_ref) | copy-start | bytes 6148
  324.8 9.7 %copy-start.5 = (f32[256,128]{1,0:T(8,128)S(1)}, f32[256,128]{1,0:T(8,128)}, u32[]{:S(2)}) copy-start(f32[256,128]{1,0:T(8,128)} %get-tuple-element.48) | copy-start | bytes 393220
  324.8 208.7 %all-to-all-start = ((bf16[16,48,1536]{2,1,0:T(8,128)(2,1)}), bf16[16,48,1536]{2,1,0:T(8,128)(2,1)}, u32[]{:S(2)}, u32[]{:S(2)}) async-start(bf16[16,48,1536]{2,1,0:T(8,128)(2,1)} %get-tuple-element.54), calls=%async_computation | async-start | bytes 4718592 | tf_op jit(solution)/shard_map/all_to_all | solution.py:1672
  332.7 3.9 copy-start
  336.6 2.7 copy-start.4
  339.3 2.4 copy-start.3
  342.2 5.2 copy-start.1
